TPU v7x, 128 devices: a whole 4x4x4 slice. The times are simulated.
128 devices in a mesh: student: 4 (over x_lo, core), ctx: 32 (over x_hi, z, y).
Axes of the slice: x: 4 (x_hi: 2, x_lo: 2; x = x_hi * 2 + x_lo), y: 4, z: 4, core: 2. Of those that a mesh axis runs over, the one named last changes fastest.
Arguments:
- query_states: bfloat16 [4, 8192, 2048], P('student', 'ctx'), may hold values from -30 to 30
- key_states: bfloat16 [4, 8192, 512], P('student', 'ctx'), may hold values from -7 to 7
- value_states: bfloat16 [4, 8192, 512], P('student', 'ctx'), may hold values from -6 to 6
- layer_inputs: bfloat16 [4, 8192, 2048], P('student', 'ctx'), may hold values from -6 to 6
- out_weight: bfloat16 [4, 2048, 2048], P('student'), may hold values from -0.5 to 0.5
- teacher: bfloat16 [8192, 8192], P('ctx', 'student'), may hold values from -6 to 6
- teacher_map: bfloat16 [8192, 2048], P('student'), may hold values from -0.0625 to 0.0625
- offsets: int32 [64], replicated, may hold values from 0 to 8064, as said below
Outputs:
- student_hidden: bfloat16 [4, 8192, 2048], P('student', 'ctx')
- weight_grad: float32 [4, 2048, 2048], P('student', 'ctx')
Inputs may be any that keep to these rules, and one draw needn't show every extreme that they name: offsets is a permutation of the 64 values 0, 128, 256, ..., 8064.
All inputs are finite; a program needn't handle non-finite values.
Results may differ from a plain program's by a relative error of at most 0.0037.
Values may be sent and summed in bfloat16 or wider, within the bound.
A program may use at most 128 MiB of HBM per device.

v0:
```python
import math

import jax
import jax.numpy as jnp
from jax import lax
from jax.sharding import PartitionSpec as P

HQ = 16
HK = 4
HD = 128


def positions_of(offsets, start, count, block_len):
    row_ids = start + jnp.arange(count, dtype=jnp.int32)
    block_ids = row_ids // block_len
    table_ids = jnp.arange(offsets.shape[0], dtype=jnp.int32)
    picked = jnp.where(block_ids[:, None] == table_ids[None, :], offsets[None, :], 0)
    return jnp.sum(picked, axis=1) + row_ids % block_len


def attention(query_local, key_local, value_local, offsets, query_pos, block_len):
    rows_here = query_local.shape[0]
    group = HQ // HK
    scale_att = HD ** (-0.5)
    query_grouped = query_local.reshape(rows_here, HK, group, HD)
    init = (
        jnp.full((HK, group, rows_here), -1e30, jnp.float32),
        jnp.zeros((HK, group, rows_here), jnp.float32),
        jnp.zeros((HK, group, rows_here, HD), jnp.float32),
    )
    key_piece = lax.all_gather(key_local, "ctx", axis=0, tiled=True)
    value_piece = lax.all_gather(value_local, "ctx", axis=0, tiled=True)
    count = key_piece.shape[0]
    width = math.gcd(count, 512)
    number = count // width
    key_blocks = key_piece.reshape(number, width, HK, HD)
    value_blocks = value_piece.reshape(number, width, HK, HD)
    key_pos = positions_of(offsets, jnp.int32(0), count, block_len).reshape(number, width)

    def one_block(state, blocks):
        run_max, run_total, run_acc = state
        key_block, value_block, pos_block = blocks
        scores = (
            jnp.einsum(
                "qhgd,khd->hgqk", query_grouped, key_block, preferred_element_type=jnp.float32
            )
            * scale_att
        )
        allowed = (pos_block[None, :] <= query_pos[:, None])[None, None]
        block_max = jnp.max(jnp.where(allowed, scores, -1e30), axis=-1)
        new_max = jnp.maximum(run_max, block_max)
        expo = jnp.where(allowed, jnp.exp(scores - new_max[..., None]), 0.0)
        factor = jnp.exp(run_max - new_max)
        new_total = run_total * factor + jnp.sum(expo, axis=-1)
        added = jnp.einsum(
            "hgqk,khd->hgqd", expo, value_block.astype(jnp.float32), precision=lax.Precision.HIGHEST
        )
        new_acc = run_acc * factor[..., None] + added
        return ((new_max, new_total, new_acc), None)

    result, _ = lax.scan(one_block, init, (key_blocks, value_blocks, key_pos))
    normed = result[2] / result[1][..., None]
    return jnp.transpose(normed, (2, 0, 1, 3)).reshape(rows_here, HQ * HD).astype(jnp.bfloat16)


def mapped_target(teacher, teacher_map):
    partial_map = jnp.dot(teacher, teacher_map, preferred_element_type=jnp.float32)
    return lax.psum(partial_map, "student")


def local(
    query_states, key_states, value_states, layer_inputs, out_weight, teacher, teacher_map, offsets
):
    query_local = query_states[0]
    rows_here = query_local.shape[0]
    block_len = rows_here // 2
    n_ctx = lax.axis_size("ctx")
    my_index = lax.axis_index("ctx")
    query_pos = positions_of(offsets, my_index * rows_here, rows_here, block_len)
    attended = attention(query_local, key_states[0], value_states[0], offsets, query_pos, block_len)
    target = mapped_target(teacher, teacher_map)
    student_f32 = layer_inputs[0].astype(jnp.float32) + jnp.dot(
        attended, out_weight[0], preferred_element_type=jnp.float32
    )
    student_hidden = student_f32.astype(jnp.bfloat16)
    scale_err = 1.0 / math.sqrt(rows_here * n_ctx)
    match_grad = ((student_f32 - target) * scale_err).astype(jnp.bfloat16)
    weight_grad = lax.psum_scatter(
        lax.dot_general(
            attended, match_grad, (((0,), (0,)), ((), ())), preferred_element_type=jnp.float32
        ),
        "ctx",
        scatter_dimension=0,
        tiled=True,
    )
    return (student_hidden[None], weight_grad[None])


def solution(mesh):
    return jax.shard_map(
        local,
        mesh=mesh,
        in_specs=(
            P("student", "ctx", None),
            P("student", "ctx", None),
            P("student", "ctx", None),
            P("student", "ctx", None),
            P("student", None, None),
            P("ctx", "student"),
            P("student", None),
            P(),
        ),
        out_specs=(P("student", "ctx", None), P("student", "ctx", None)),
        check_vma=False,
    )
```

profile of v0, /device:TPU:2, one launch (start us, length us, event | category | flops | bytes accessed | tf_op | source)
XLA Modules:
  0.0 841.6 jit_solution(14836105789162001493)
XLA Ops:
  9.6 7.1 fusion.32
  18.6 101.7 %all-gather.5.cloned.1.call-done = bf16[1,8192,512]{2,1,0:T(8,128)(2,1)} async-done(((bf16[1,256,512]{2,1,0:T(8,128)(2,1)}), bf16[1,8192,512]{2,1,0:T(8,128)(2,1)}) %all-gather.5.cloned.1.call-update) | async-done | bytes 8388624 | tf_op jit(solution)/shard_map/all_gather | solution.py:31
  120.3 12.6 %reshape.91 = bf16[16,512,4,128]{3,2,1,0:T(4,128)(2,1)} reshape(bf16[1,8192,512]{2,1,0:T(8,128)(2,1)} %all-gather.5.cloned.1.call-done) | data formatting | bytes 16777216 | tf_op jit(solution)/shard_map/reshape | solution.py:36
  132.8 92.3 %all-gather.7.cloned.1.call-done = bf16[1,8192,512]{2,1,0:T(8,128)(2,1)} async-done(((bf16[1,256,512]{2,1,0:T(8,128)(2,1)}), bf16[1,8192,512]{2,1,0:T(8,128)(2,1)}) %all-gather.7.cloned.1.call-update) | async-done | bytes 8388624 | tf_op jit(solution)/shard_map/all_gather | solution.py:32
  225.2 12.5 %reshape.92 = bf16[16,512,4,128]{3,2,1,0:T(4,128)(2,1)} reshape(bf16[1,8192,512]{2,1,0:T(8,128)(2,1)} %all-gather.7.cloned.1.call-done) | data formatting | bytes 16777216 | tf_op jit(solution)/shard_map/reshape | solution.py:37
  237.7 355.7 %while.15 = (s32[]{:T(128)}, f32[4,4,256]{2,1,0:T(4,128)S(1)}, f32[4,4,256]{2,1,0:T(4,128)S(1)}, f32[4,4,256,128]{3,2,1,0:T(8,128)}, s32[16,512]{1,0:T(8,128)S(1...) while((s32[]{:T(128)}, f32[4,4,256]{2,1,0:T(4,128)S(1)}, ...), condition=%wide.region_5.6_spmd.clone, body=%wide.region_2.5_spmd.clone.sunk | while | flops 3780792320 | bytes 67902624 | solution.py:61
  249.8 8.9 %fusion.49 = f32[4,4,256,128]{3,2,1,0:T(8,128)} fusion(f32[4,4,256,128]{3,2,1,0:T(8,128)} %get-tuple-element.205, f32[4,512,256,4]{2,1,3,0:T(8,128)S(1)} %copy-done.2, f32[4,4,256]{2,1,0:T(4,128)S(1)} %select_maximum_fusion.2, pred[256,512]{0,1:T(8,128)(4,1)S(1)} %broadcast_compare_fusion.3, f32[4,4,256]{2,1,0:T(4,128)S(1)} %get-tuple-element.189, ...), kind=kOutput, calls=%fused_computation.12.clone.1 | convolution fusion | flops 3229089792 | bytes 13271041 | tf_op jit(solution)/shard_map/while/body/eval_jaxpr/hgqk,khd->hgqd/dot_general | solution.py:55
  270.9 10.1 %fusion.49 = f32[4,4,256,128]{3,2,1,0:T(8,128)} fusion(f32[4,4,256,128]{3,2,1,0:T(8,128)} %get-tuple-element.205, f32[4,512,256,4]{2,1,3,0:T(8,128)S(1)} %copy-done.2, f32[4,4,256]{2,1,0:T(4,128)S(1)} %select_maximum_fusion.2, pred[256,512]{0,1:T(8,128)(4,1)S(1)} %broadcast_compare_fusion.3, f32[4,4,256]{2,1,0:T(4,128)S(1)} %get-tuple-element.189, ...), kind=kOutput, calls=%fused_computation.12.clone.1 | convolution fusion | flops 3229089792 | bytes 13271041 | tf_op jit(solution)/shard_map/while/body/eval_jaxpr/hgqk,khd->hgqd/dot_general | solution.py:55
  293.2 10.1 %fusion.49 = f32[4,4,256,128]{3,2,1,0:T(8,128)} fusion(f32[4,4,256,128]{3,2,1,0:T(8,128)} %get-tuple-element.205, f32[4,512,256,4]{2,1,3,0:T(8,128)S(1)} %copy-done.2, f32[4,4,256]{2,1,0:T(4,128)S(1)} %select_maximum_fusion.2, pred[256,512]{0,1:T(8,128)(4,1)S(1)} %broadcast_compare_fusion.3, f32[4,4,256]{2,1,0:T(4,128)S(1)} %get-tuple-element.189, ...), kind=kOutput, calls=%fused_computation.12.clone.1 | convolution fusion | flops 3229089792 | bytes 13271041 | tf_op jit(solution)/shard_map/while/body/eval_jaxpr/hgqk,khd->hgqd/dot_general | solution.py:55
  315.6 10.1 %fusion.49 = f32[4,4,256,128]{3,2,1,0:T(8,128)} fusion(f32[4,4,256,128]{3,2,1,0:T(8,128)} %get-tuple-element.205, f32[4,512,256,4]{2,1,3,0:T(8,128)S(1)} %copy-done.2, f32[4,4,256]{2,1,0:T(4,128)S(1)} %select_maximum_fusion.2, pred[256,512]{0,1:T(8,128)(4,1)S(1)} %broadcast_compare_fusion.3, f32[4,4,256]{2,1,0:T(4,128)S(1)} %get-tuple-element.189, ...), kind=kOutput, calls=%fused_computation.12.clone.1 | convolution fusion | flops 3229089792 | bytes 13271041 | tf_op jit(solution)/shard_map/while/body/eval_jaxpr/hgqk,khd->hgqd/dot_general | solution.py:55
  337.9 10.1 %fusion.49 = f32[4,4,256,128]{3,2,1,0:T(8,128)} fusion(f32[4,4,256,128]{3,2,1,0:T(8,128)} %get-tuple-element.205, f32[4,512,256,4]{2,1,3,0:T(8,128)S(1)} %copy-done.2, f32[4,4,256]{2,1,0:T(4,128)S(1)} %select_maximum_fusion.2, pred[256,512]{0,1:T(8,128)(4,1)S(1)} %broadcast_compare_fusion.3, f32[4,4,256]{2,1,0:T(4,128)S(1)} %get-tuple-element.189, ...), kind=kOutput, calls=%fused_computation.12.clone.1 | convolution fusion | flops 3229089792 | bytes 13271041 | tf_op jit(solution)/shard_map/while/body/eval_jaxpr/hgqk,khd->hgqd/dot_general | solution.py:55
  360.2 10.1 %fusion.49 = f32[4,4,256,128]{3,2,1,0:T(8,128)} fusion(f32[4,4,256,128]{3,2,1,0:T(8,128)} %get-tuple-element.205, f32[4,512,256,4]{2,1,3,0:T(8,128)S(1)} %copy-done.2, f32[4,4,256]{2,1,0:T(4,128)S(1)} %select_maximum_fusion.2, pred[256,512]{0,1:T(8,128)(4,1)S(1)} %broadcast_compare_fusion.3, f32[4,4,256]{2,1,0:T(4,128)S(1)} %get-tuple-element.189, ...), kind=kOutput, calls=%fused_computation.12.clone.1 | convolution fusion | flops 3229089792 | bytes 13271041 | tf_op jit(solution)/shard_map/while/body/eval_jaxpr/hgqk,khd->hgqd/dot_general | solution.py:55
  382.5 10.1 %fusion.49 = f32[4,4,256,128]{3,2,1,0:T(8,128)} fusion(f32[4,4,256,128]{3,2,1,0:T(8,128)} %get-tuple-element.205, f32[4,512,256,4]{2,1,3,0:T(8,128)S(1)} %copy-done.2, f32[4,4,256]{2,1,0:T(4,128)S(1)} %select_maximum_fusion.2, pred[256,512]{0,1:T(8,128)(4,1)S(1)} %broadcast_compare_fusion.3, f32[4,4,256]{2,1,0:T(4,128)S(1)} %get-tuple-element.189, ...), kind=kOutput, calls=%fused_computation.12.clone.1 | convolution fusion | flops 3229089792 | bytes 13271041 | tf_op jit(solution)/shard_map/while/body/eval_jaxpr/hgqk,khd->hgqd/dot_general | solution.py:55
  404.8 10.1 %fusion.49 = f32[4,4,256,128]{3,2,1,0:T(8,128)} fusion(f32[4,4,256,128]{3,2,1,0:T(8,128)} %get-tuple-element.205, f32[4,512,256,4]{2,1,3,0:T(8,128)S(1)} %copy-done.2, f32[4,4,256]{2,1,0:T(4,128)S(1)} %select_maximum_fusion.2, pred[256,512]{0,1:T(8,128)(4,1)S(1)} %broadcast_compare_fusion.3, f32[4,4,256]{2,1,0:T(4,128)S(1)} %get-tuple-element.189, ...), kind=kOutput, calls=%fused_computation.12.clone.1 | convolution fusion | flops 3229089792 | bytes 13271041 | tf_op jit(solution)/shard_map/while/body/eval_jaxpr/hgqk,khd->hgqd/dot_general | solution.py:55
  427.1 10.1 %fusion.49 = f32[4,4,256,128]{3,2,1,0:T(8,128)} fusion(f32[4,4,256,128]{3,2,1,0:T(8,128)} %get-tuple-element.205, f32[4,512,256,4]{2,1,3,0:T(8,128)S(1)} %copy-done.2, f32[4,4,256]{2,1,0:T(4,128)S(1)} %select_maximum_fusion.2, pred[256,512]{0,1:T(8,128)(4,1)S(1)} %broadcast_compare_fusion.3, f32[4,4,256]{2,1,0:T(4,128)S(1)} %get-tuple-element.189, ...), kind=kOutput, calls=%fused_computation.12.clone.1 | convolution fusion | flops 3229089792 | bytes 13271041 | tf_op jit(solution)/shard_map/while/body/eval_jaxpr/hgqk,khd->hgqd/dot_general | solution.py:55
  449.4 10.1 %fusion.49 = f32[4,4,256,128]{3,2,1,0:T(8,128)} fusion(f32[4,4,256,128]{3,2,1,0:T(8,128)} %get-tuple-element.205, f32[4,512,256,4]{2,1,3,0:T(8,128)S(1)} %copy-done.2, f32[4,4,256]{2,1,0:T(4,128)S(1)} %select_maximum_fusion.2, pred[256,512]{0,1:T(8,128)(4,1)S(1)} %broadcast_compare_fusion.3, f32[4,4,256]{2,1,0:T(4,128)S(1)} %get-tuple-element.189, ...), kind=kOutput, calls=%fused_computation.12.clone.1 | convolution fusion | flops 3229089792 | bytes 13271041 | tf_op jit(solution)/shard_map/while/body/eval_jaxpr/hgqk,khd->hgqd/dot_general | solution.py:55
  471.7 10.1 %fusion.49 = f32[4,4,256,128]{3,2,1,0:T(8,128)} fusion(f32[4,4,256,128]{3,2,1,0:T(8,128)} %get-tuple-element.205, f32[4,512,256,4]{2,1,3,0:T(8,128)S(1)} %copy-done.2, f32[4,4,256]{2,1,0:T(4,128)S(1)} %select_maximum_fusion.2, pred[256,512]{0,1:T(8,128)(4,1)S(1)} %broadcast_compare_fusion.3, f32[4,4,256]{2,1,0:T(4,128)S(1)} %get-tuple-element.189, ...), kind=kOutput, calls=%fused_computation.12.clone.1 | convolution fusion | flops 3229089792 | bytes 13271041 | tf_op jit(solution)/shard_map/while/body/eval_jaxpr/hgqk,khd->hgqd/dot_general | solution.py:55
  494.0 10.1 %fusion.49 = f32[4,4,256,128]{3,2,1,0:T(8,128)} fusion(f32[4,4,256,128]{3,2,1,0:T(8,128)} %get-tuple-element.205, f32[4,512,256,4]{2,1,3,0:T(8,128)S(1)} %copy-done.2, f32[4,4,256]{2,1,0:T(4,128)S(1)} %select_maximum_fusion.2, pred[256,512]{0,1:T(8,128)(4,1)S(1)} %broadcast_compare_fusion.3, f32[4,4,256]{2,1,0:T(4,128)S(1)} %get-tuple-element.189, ...), kind=kOutput, calls=%fused_computation.12.clone.1 | convolution fusion | flops 3229089792 | bytes 13271041 | tf_op jit(solution)/shard_map/while/body/eval_jaxpr/hgqk,khd->hgqd/dot_general | solution.py:55
  516.3 10.1 %fusion.49 = f32[4,4,256,128]{3,2,1,0:T(8,128)} fusion(f32[4,4,256,128]{3,2,1,0:T(8,128)} %get-tuple-element.205, f32[4,512,256,4]{2,1,3,0:T(8,128)S(1)} %copy-done.2, f32[4,4,256]{2,1,0:T(4,128)S(1)} %select_maximum_fusion.2, pred[256,512]{0,1:T(8,128)(4,1)S(1)} %broadcast_compare_fusion.3, f32[4,4,256]{2,1,0:T(4,128)S(1)} %get-tuple-element.189, ...), kind=kOutput, calls=%fused_computation.12.clone.1 | convolution fusion | flops 3229089792 | bytes 13271041 | tf_op jit(solution)/shard_map/while/body/eval_jaxpr/hgqk,khd->hgqd/dot_general | solution.py:55
  538.6 10.1 %fusion.49 = f32[4,4,256,128]{3,2,1,0:T(8,128)} fusion(f32[4,4,256,128]{3,2,1,0:T(8,128)} %get-tuple-element.205, f32[4,512,256,4]{2,1,3,0:T(8,128)S(1)} %copy-done.2, f32[4,4,256]{2,1,0:T(4,128)S(1)} %select_maximum_fusion.2, pred[256,512]{0,1:T(8,128)(4,1)S(1)} %broadcast_compare_fusion.3, f32[4,4,256]{2,1,0:T(4,128)S(1)} %get-tuple-element.189, ...), kind=kOutput, calls=%fused_computation.12.clone.1 | convolution fusion | flops 3229089792 | bytes 13271041 | tf_op jit(solution)/shard_map/while/body/eval_jaxpr/hgqk,khd->hgqd/dot_general | solution.py:55
  560.9 10.1 %fusion.49 = f32[4,4,256,128]{3,2,1,0:T(8,128)} fusion(f32[4,4,256,128]{3,2,1,0:T(8,128)} %get-tuple-element.205, f32[4,512,256,4]{2,1,3,0:T(8,128)S(1)} %copy-done.2, f32[4,4,256]{2,1,0:T(4,128)S(1)} %select_maximum_fusion.2, pred[256,512]{0,1:T(8,128)(4,1)S(1)} %broadcast_compare_fusion.3, f32[4,4,256]{2,1,0:T(4,128)S(1)} %get-tuple-element.189, ...), kind=kOutput, calls=%fused_computation.12.clone.1 | convolution fusion | flops 3229089792 | bytes 13271041 | tf_op jit(solution)/shard_map/while/body/eval_jaxpr/hgqk,khd->hgqd/dot_general | solution.py:55
  583.2 10.1 %fusion.49 = f32[4,4,256,128]{3,2,1,0:T(8,128)} fusion(f32[4,4,256,128]{3,2,1,0:T(8,128)} %get-tuple-element.205, f32[4,512,256,4]{2,1,3,0:T(8,128)S(1)} %copy-done.2, f32[4,4,256]{2,1,0:T(4,128)S(1)} %select_maximum_fusion.2, pred[256,512]{0,1:T(8,128)(4,1)S(1)} %broadcast_compare_fusion.3, f32[4,4,256]{2,1,0:T(4,128)S(1)} %get-tuple-element.189, ...), kind=kOutput, calls=%fused_computation.12.clone.1 | convolution fusion | flops 3229089792 | bytes 13271041 | tf_op jit(solution)/shard_map/while/body/eval_jaxpr/hgqk,khd->hgqd/dot_general | solution.py:55
  601.7 9.7 %fusion.22 = f32[2048,2048]{1,0:T(8,128)} fusion(bf16[256,2048]{0,1:T(8,128)(2,1)S(1)} %bitcast.64, f32[256,2048]{1,0:T(8,128)S(1)} %fusion.19, f32[256,2048]{1,0:T(8,128)} %all-reduce.2.cloned.1.call-done), kind=kOutput, calls=%fused_computation.33 | convolution fusion | flops 2149056512 | bytes 22020096 | tf_op jit(solution)/shard_map/dot_general | solution.py:89
  612.5 222.0 %reduce-scatter.2.cloned.1.call-done = f32[64,2048]{1,0:T(8,128)} async-done(((f32[2048,2048]{1,0:T(8,128)}), f32[64,2048]{1,0:T(8,128)}) %reduce-scatter.2.cloned.1.call-update) | async-done | bytes 524304 | tf_op jit(solution)/shard_map/reduce_scatter | solution.py:88
  (193 shorter events, 207.0 us)
Async XLA Ops:
  8.0 1.6 copy-start
  8.0 112.3 %all-gather.5.cloned.1.call-start = ((), (), s32[]{:S(2)}) async-start(), calls=%async_computation.3 | async-start | bytes 8650752 | tf_op jit(solution)/shard_map/all_gather | solution.py:31
  8.7 216.4 %all-gather.7.cloned.1.call-start = ((), (), s32[]{:S(2)}) async-start(), calls=%async_computation.4 | async-start | bytes 8650752 | tf_op jit(solution)/shard_map/all_gather | solution.py:32
  9.5 7.3 copy-start.4
  9.5 7.4 copy-start.3
  9.5 592.2 %all-reduce.2.cloned.1.call-start = ((), (), s32[]{:S(2)}) async-start(), calls=%async_computation.1 | async-start | bytes 4194304 | tf_op jit(solution)/shard_map/psum | solution.py:68
  16.7 817.8 %reduce-scatter.2.cloned.1.call-start = ((), (), s32[]{:S(2)}) async-start(), calls=%async_computation.2 | async-start | bytes 17301504 | tf_op jit(solution)/shard_map/reduce_scatter | solution.py:88
  244.1 5.8 copy-start.2
  265.2 5.8 copy-start.2
  287.5 5.8 copy-start.2
  309.8 5.8 copy-start.2
  332.1 5.8 copy-start.2
  354.4 5.8 copy-start.2
  376.7 5.8 copy-start.2
  399.0 5.8 copy-start.2
  421.3 5.8 copy-start.2
  443.6 5.8 copy-start.2
  465.9 5.8 copy-start.2
  488.2 5.8 copy-start.2
  510.5 5.8 copy-start.2
  532.9 5.8 copy-start.2
  555.2 5.8 copy-start.2
  577.5 5.8 copy-start.2
  611.4 223.1 %copy-start.1 = (bf16[256,2048]{1,0:T(8,128)(2,1)S(1)}, bf16[256,2048]{1,0:T(8,128)(2,1)}, u32[]{:S(2)}) copy-start(bf16[256,2048]{1,0:T(8,128)(2,1)} %param.15) | copy-start | bytes 3145732
Sparse Core Ops, SparseCore 0:
  11.9 108.3 all-gather.4
  123.3 101.7 all-gather.6
  611.5 222.9 reduce-scatter.1
Sparse Core Ops, SparseCore 1:
  16.8 58.0 all-reduce.1
where the time goes:
time: 843 us; the launch traced here: 842 us
  waiting for transfers between devices  417 us (49%)
  matrix products  258 us (31%)
  other arithmetic  88.7 us (11%)
  local copies, waits for them, and re-layouts  61.2 us (7%)
  between operations  15.3 us (2%)
    reduce_scatter x1, waiting for transfers between devices, local(): lax.psum_scatter(lax.dot_general(attended, match_grad, (((0,), (0,)), (()...  222 us
    dot_general x16, matrix products, one_block(): jnp.einsum('hgqk,khd->hgqd', expo, value_block.astype(jnp.float32), preci...  161 us
    all_gather x1, waiting for transfers between devices, attention(): key_piece = lax.all_gather(key_local, 'ctx', axis=0, tiled=True)  102 us
    all_gather x1, waiting for transfers between devices, attention(): value_piece = lax.all_gather(value_local, 'ctx', axis=0, tiled=True)  92.3 us
    reduce_sum x16, other arithmetic, one_block(): new_total = run_total * factor + jnp.sum(expo, axis=-1)  84 us
    dot_general x16, matrix products, one_block(): jnp.einsum('qhgd,khd->hgqk', query_grouped, key_block, preferred_element_...  74.6 us
    dynamic_slice x32, local copies, waits for them, and re-layouts, attention(): result, _ = lax.scan(one_block, init, (key_blocks, value_blocks, key_pos))  25.2 us
  transfers between devices with their start and end apart: 4, of which 3 were waited for; matrix products, arithmetic and copies ran while one was open for 46% of the time, Pallas kernels for 0%

commit v1 on v0

v1 whole, which is shorter than its diff:
```python
import math

import jax
import jax.numpy as jnp
from jax import lax
from jax.experimental import pallas as pl
from jax.experimental.pallas import tpu as pltpu
from jax.sharding import PartitionSpec as P

F32 = jnp.float32
BF16 = jnp.bfloat16
N = 32
HD = 128
SCALE = HD**-0.5 * math.log2(math.e)
ERR = 1.0 / math.sqrt(8192.0)
NEG = -1e30
GROUPS = 8
M = 512
CW = 1024
MESH = pl.DeviceIdType.MESH


def kernel(
    q, k, v, li, w, te, tm, order,
    sh_out, wg_out,
    li_v, w_v, te_v, tm_v, kv, q_recv, qp, kpos, vp, att, d_home, d_recv, dpos,
    tp, tx, tt, th, th_recv, mg, aw, sh_send, sh_recv, wg_send, wg_recv,
    sa, sb, m_ref, acc,
    loc, loc_tm, s1_s, s1_r, g_s, g_r, x_s, x_r, q_s, q_r, t_s, t_r, d_s, d_r,
    ag_s, ag_r, sh_s, sh_r, wg_s, wg_r,
):
    stu = lax.axis_index("student")
    me = lax.axis_index("ctx")
    core = lax.rem(stu, 2)
    xlo = stu // 2
    xh = me // 16
    mid, low = lax.rem(me // 4, 4), lax.rem(me, 4)
    a = jnp.where(core == 0, low, mid)
    b = jnp.where(core == 0, mid, low)
    t = xh * 4 + b
    mine = xh * 16 + b * 4 + a

    def ctx_of(x_, a_, b_):
        return x_ * 16 + jnp.where(core == 0, b_ * 4 + a_, a_ * 4 + b_)

    def remote(src, dst, ss, rs, where):
        return pltpu.make_async_remote_copy(
            src_ref=src, dst_ref=dst, send_sem=ss, recv_sem=rs, device_id=where, device_id_type=MESH
        )

    def cols(i, width):
        return pl.ds(pl.multiple_of(i * width, width), width)

    def peer(kk, sign):
        dx, db, da = kk // 16, lax.rem(kk // 4, 4), lax.rem(kk, 4)
        x_ = lax.rem(xh + dx, 2)
        a_ = lax.rem(a + sign * da + 4, 4)
        b_ = lax.rem(b + sign * db + 4, 4)
        return x_, a_, b_

    tm_loads = [
        pltpu.make_async_copy(tm.at[:, pl.ds(512 * i, 512)], tm_v.at[i % 2], loc_tm.at[i % 2])
        for i in range(4)
    ]
    c_te = pltpu.make_async_copy(te, te_v, loc.at[0])
    c_li = pltpu.make_async_copy(li, li_v, loc.at[1])
    c_w = pltpu.make_async_copy(w.at[:, cols(a, 512)], w_v, loc.at[2])
    c_k = pltpu.make_async_copy(k.at[:, :, cols(a, HD)], kv.at[mine, 0], loc.at[3])
    c_v = pltpu.make_async_copy(v.at[:, :, cols(a, HD)], kv.at[mine, 1], loc.at[4])
    c_q = pltpu.make_async_copy(q.at[:, cols(t, 16), cols(a, 512)], q_recv.at[mine], loc.at[5])
    for c in (c_k, c_v, c_q, c_te, tm_loads[0], tm_loads[1], c_li, c_w):
        c.start()

    barrier = pltpu.get_barrier_semaphore()

    def greet(i, _):
        pl.semaphore_signal(barrier, inc=1, device_id={"ctx": lax.rem(me + i, N)}, device_id_type=MESH)
        return 0

    lax.fori_loop(1, N, greet, 0)
    pair_core = {"student": xlo * 2 + 1 - core}
    pair_xlo = {"student": (1 - xlo) * 2 + core}
    pl.semaphore_signal(barrier, inc=1, device_id=pair_core, device_id_type=MESH)
    pl.semaphore_signal(barrier, inc=1, device_id=pair_xlo, device_id_type=MESH)
    pl.semaphore_wait(barrier, N + 1)

    firsts = []
    for da in range(1, 4):
        to = lax.rem(a + da, 4)
        for i, src in enumerate((k, v)):
            firsts.append(
                remote(
                    src.at[:, :, cols(to, HD)], kv.at[mine, i], s1_s.at[da, i], s1_r.at[da, i],
                    {"ctx": ctx_of(xh, to, b)},
                )
            )
    for c in firsts:
        c.start()

    def q_copy(kk, sign=1):
        x_, a_, b_ = peer(kk, sign)
        return remote(
            q.at[:, cols(x_ * 4 + b_, 16), cols(a_, 512)], q_recv.at[mine], q_s.at[kk], q_r.at[kk],
            {"ctx": ctx_of(x_, a_, b_)},
        )

    def q_start(kk, _):
        q_copy(kk).start()
        return 0

    lax.fori_loop(1, N, q_start, 0)
    c_k.wait()
    c_v.wait()
    for da in range(1, 4):
        frm = lax.rem(a - da + 4, 4)
        for i in range(2):
            at = kv.at[xh * 16 + b * 4 + frm, i]
            remote(at, at, s1_s.at[da, i], s1_r.at[da, i], {"ctx": ctx_of(xh, frm, b)}).wait_recv()
    own = kv.at[pl.ds(xh * 16 + b * 4, 4)]
    other = kv.at[pl.ds((1 - xh) * 16 + b * 4, 4)]
    seconds = [remote(own, own, g_s.at[0], g_r.at[0], {"ctx": ctx_of(1 - xh, a, b)})]
    for db in range(1, 4):
        seconds.append(
            remote(own, own, g_s.at[db], g_r.at[db], {"ctx": ctx_of(xh, a, lax.rem(b + db, 4))})
        )
    for c in seconds:
        c.start()

    vp[:, HD:] = jnp.ones((8192, HD), BF16)
    c_te.wait()
    for i in range(4):
        tm_loads[i].wait()
        tp[:, 512 * i : 512 * i + 512] = jnp.dot(te_v[...], tm_v[i % 2], preferred_element_type=F32)
        if i < 2:
            tm_loads[i + 2].start()
    half = pl.ds(pl.multiple_of(core * 128, 128), 128)
    half2 = pl.ds(pl.multiple_of((1 - core) * 128, 128), 128)
    t1 = remote(tp.at[half2], tx, t_s.at[0], t_r.at[0], pair_core)
    t1.start()
    t1.wait()
    th[...] = (tp[half, :] + tx[...]).astype(BF16)
    t2 = remote(th, th_recv, t_s.at[1], t_r.at[1], pair_xlo)
    t2.start()

    remote(other, other, g_s.at[0], g_r.at[0], {"ctx": ctx_of(1 - xh, a, b)}).wait_recv()
    thirds = []
    for db in range(1, 4):
        thirds.append(
            remote(other, other, x_s.at[db], x_r.at[db], {"ctx": ctx_of(xh, a, lax.rem(b + db, 4))})
        )
    for c in thirds:
        c.start()
    t2.wait()
    tp[half, :] = tp[half, :] + tx[...] + th_recv[...].astype(F32)
    t3 = remote(tp.at[half], tt, t_s.at[2], t_r.at[2], pair_core)
    t3.start()
    c_li.wait()
    d_home[core] = (li_v[core].astype(F32) - tp[half, :]).astype(BF16)
    t3.wait()
    d_home[1 - core] = (li_v[1 - core].astype(F32) - tt[...]).astype(BF16)

    c_q.wait()

    def q_wait(kk, _):
        x_, a_, b_ = peer(kk, -1)
        at = q_recv.at[x_ * 16 + b_ * 4 + a_]
        remote(at, at, q_s.at[kk], q_r.at[kk], {"ctx": ctx_of(x_, a_, b_)}).wait_recv()
        return 0

    lax.fori_loop(1, N, q_wait, 0)
    for db in range(1, 4):
        frm = lax.rem(b - db + 4, 4)
        at = kv.at[pl.ds(xh * 16 + frm * 4, 4)]
        remote(at, at, g_s.at[db], g_r.at[db], {"ctx": ctx_of(xh, a, frm)}).wait_recv()
        at = kv.at[pl.ds((1 - xh) * 16 + frm * 4, 4)]
        remote(at, at, x_s.at[db], x_r.at[db], {"ctx": ctx_of(xh, a, frm)}).wait_recv()

    def d_copy(kk):
        x_, a_, b_ = peer(kk, 1)
        return remote(
            d_home.at[:, cols(x_ * 4 + b_, 16), cols(a_, 512)], d_recv.at[mine], d_s.at[kk], d_r.at[kk],
            {"ctx": ctx_of(x_, a_, b_)},
        )

    def d_start(kk, _):
        d_copy(kk).start()
        return 0

    lax.fori_loop(1, N, d_start, 0)
    d_recv[mine] = d_home[:, cols(t, 16), cols(a, 512)]

    def arrange(p, _):
        at = order[64 + p]
        part = order[128 + p]
        to = pl.ds(pl.multiple_of(p * 128, 128), 128)
        kpos[to, :] = kv[at, 0, part]
        vp[to, :HD] = kv[at, 1, part]
        slab = q_recv[at, part]
        for h in range(4):
            qp[p // 8, h, pl.ds(pl.multiple_of(lax.rem(p, 8) * 16, 16), 16), :] = slab[:, h * HD : h * HD + HD]
        return 0

    lax.fori_loop(0, 64, arrange, 0)

    def score(g, j, dst):
        dst[...] = lax.dot_general(
            qp[g].reshape(M, HD), kpos[cols(j, CW), :], (((1,), (1,)), ((), ())), preferred_element_type=F32
        )

    def absorb(src, j, diagonal=False):
        s = src[...]
        if diagonal:
            row = lax.rem(lax.broadcasted_iota(jnp.int32, (M, CW), 0), 128)
            col = lax.broadcasted_iota(jnp.int32, (M, CW), 1)
            s = jnp.where(col <= (row // 16) * 128 + t * 16 + lax.rem(row, 16), s, NEG)
        old = m_ref[...]
        new = jnp.maximum(old, jnp.max(s, axis=1, keepdims=True))
        m_ref[...] = new
        factor = jnp.exp2((old - new) * SCALE)
        p = jnp.exp2(s * SCALE - jnp.tile(new * SCALE, (1, CW // 128))).astype(BF16)
        acc[...] = acc[...] * jnp.tile(factor, (1, 2)) + jnp.dot(
            p, vp[cols(j, CW), :], preferred_element_type=F32
        )

    def begin():
        m_ref[...] = jnp.full((M, 128), NEG, F32)
        acc[...] = jnp.zeros((M, 256), F32)

    def att_copy(g, da):
        at = att.at[cols(g, 128), cols(a, 512)]
        return remote(at, at, ag_s.at[g, da], ag_r.at[g, da], {"ctx": ctx_of(xh, lax.rem(a + da, 4), b)})

    def finish(g):
        for h in range(4):
            rows = slice(h * 128, h * 128 + 128)
            att[cols(g, 128), pl.ds(pl.multiple_of(a * 512 + h * 128, 128), 128)] = (
                acc[rows, :HD] / acc[rows, HD:]
            ).astype(BF16)
        for da in range(1, 4):
            att_copy(g, da).start()

    def two_groups(u, _):
        g = 2 * u
        begin()
        score(g, 0, sa)

        def even(i, _):
            score(g, 2 * i + 1, sb)
            absorb(sa, 2 * i)
            score(g, 2 * i + 2, sa)
            absorb(sb, 2 * i + 1)
            return 0

        lax.fori_loop(0, u, even, 0)
        score(g + 1, 0, sb)
        absorb(sa, g, True)
        finish(g)
        begin()

        def odd(i, _):
            score(g + 1, 2 * i + 1, sa)
            absorb(sb, 2 * i)
            score(g + 1, 2 * i + 2, sb)
            absorb(sa, 2 * i + 1)
            return 0

        lax.fori_loop(0, u, odd, 0)
        score(g + 1, g + 1, sa)
        absorb(sb, g)
        absorb(sa, g + 1, True)
        finish(g + 1)
        return 0

    lax.fori_loop(0, GROUPS // 2, two_groups, 0)

    def d_wait(kk, _):
        x_, a_, b_ = peer(kk, -1)
        at = d_recv.at[x_ * 16 + b_ * 4 + a_]
        remote(at, at, d_s.at[kk], d_r.at[kk], {"ctx": ctx_of(x_, a_, b_)}).wait_recv()
        return 0

    lax.fori_loop(1, N, d_wait, 0)

    def arrange_d(p, _):
        dpos[cols(p, 16), :] = d_recv[order[64 + p], order[128 + p]]
        return 0

    lax.fori_loop(0, 64, arrange_d, 0)
    c_w.wait()

    def project(i, _):
        for g2 in range(2):
            g = 2 * i + g2
            for da in range(1, 4):
                frm = lax.rem(a - da + 4, 4)
                at = att.at[cols(g, 128), cols(frm, 512)]
                remote(at, at, ag_s.at[g, da], ag_r.at[g, da], {"ctx": ctx_of(xh, frm, b)}).wait_recv()
        rows = cols(i, 256)
        x = jnp.dot(att[rows, :], w_v[...], preferred_element_type=F32)
        aw[pl.ds(16 * i, 16)] = x.astype(BF16).reshape(16, 16, 512)
        mg[rows, :] = ((x + dpos[rows, :].astype(F32)) * ERR).astype(BF16)
        return 0

    lax.fori_loop(0, 4, project, 0)

    def arrange_sh(blk, _):
        sh_send[blk // 2, lax.rem(blk, 2)] = aw[order[blk]]
        return 0

    lax.fori_loop(0, 64, arrange_sh, 0)

    def sh_copy(kk):
        x_, a_, b_ = peer(kk, 1)
        to = ctx_of(x_, a_, b_)
        return remote(
            sh_send.at[to], sh_recv.at[:, cols(t, 16), cols(a, 512)], sh_s.at[kk], sh_r.at[kk], {"ctx": to}
        )

    def sh_start(kk, _):
        sh_copy(kk).start()
        return 0

    lax.fori_loop(1, N, sh_start, 0)
    sh_recv[:, cols(t, 16), cols(a, 512)] = sh_send[me]

    def wg_copy(to):
        return remote(
            wg_send.at[to], wg_recv.at[t, :, cols(a, 512)], wg_s.at[to], wg_r.at[me], {"ctx": to}
        )

    def wgrad(i, _):
        quad = lax.rem(me // 4 + i, 8)
        part = lax.dot_general(
            att[:, cols(quad, 256)], mg[...], (((0,), (0,)), ((), ())), preferred_element_type=F32
        ).astype(BF16)
        wg_send[pl.ds(quad * 4, 4)] = part.reshape(4, 64, 512)
        for r in range(4):
            to = quad * 4 + r

            @pl.when(to != me)
            def _():
                wg_copy(to).start()

        return 0

    lax.fori_loop(0, 8, wgrad, 0)
    wg_recv[t, :, cols(a, 512)] = wg_send[me]

    def sh_wait(kk, _):
        x_, a_, b_ = peer(kk, -1)
        at = sh_recv.at[:, cols(x_ * 4 + b_, 16), cols(a_, 512)]
        remote(sh_send.at[0], at, sh_s.at[kk], sh_r.at[kk], {"ctx": ctx_of(x_, a_, b_)}).wait_recv()
        return 0

    lax.fori_loop(1, N, sh_wait, 0)
    sh_out[...] = (li_v[...].astype(F32) + sh_recv[...].astype(F32)).astype(BF16)

    def wg_wait(kk, _):
        x_, a_, b_ = peer(kk, -1)
        frm = ctx_of(x_, a_, b_)
        at = wg_recv.at[x_ * 4 + b_, :, cols(a_, 512)]
        remote(wg_send.at[0], at, wg_s.at[frm], wg_r.at[frm], {"ctx": frm}).wait_recv()
        return 0

    lax.fori_loop(1, N, wg_wait, 0)
    total = wg_recv[0].astype(F32)
    for i in range(1, 8):
        total = total + wg_recv[i].astype(F32)
    wg_out[...] = total

    for c in firsts + seconds + thirds:
        c.wait_send()

    def drain(kk, _):
        q_copy(kk).wait_send()
        d_copy(kk).wait_send()
        sh_copy(kk).wait_send()
        wg_copy(lax.rem(me + kk, N)).wait_send()
        return 0

    lax.fori_loop(1, N, drain, 0)

    def drain_att(g, _):
        for da in range(1, 4):
            att_copy(g, da).wait_send()
        return 0

    lax.fori_loop(0, GROUPS, drain_att, 0)


def local(query_states, key_states, value_states, layer_inputs, out_weight, teacher, teacher_map, offsets):
    pos = offsets // 128
    ids = jnp.arange(64, dtype=jnp.int32)
    inv = jnp.sum(jnp.where(pos[None, :] == ids[:, None], ids[None, :], 0), axis=1)
    home = inv // 2
    swapped = (home // 16) * 16 + (home % 4) * 4 + (home // 4) % 4
    slot = jnp.where(lax.axis_index("student") % 2 == 0, home, swapped)
    order = jnp.concatenate([pos, slot, inv % 2])
    hbm = pl.BlockSpec(memory_space=pl.ANY)
    vmem = pl.BlockSpec(memory_space=pltpu.VMEM)
    dma = pltpu.SemaphoreType.DMA
    sh, wg = pl.pallas_call(
        kernel,
        name="layer",
        out_shape=(
            jax.ShapeDtypeStruct((2, 128, 2048), BF16),
            jax.ShapeDtypeStruct((64, 2048), F32),
        ),
        in_specs=[hbm] * 7 + [pl.BlockSpec(memory_space=pltpu.SMEM)],
        out_specs=(vmem, vmem),
        scratch_shapes=[
            pltpu.VMEM((2, 128, 2048), BF16),
            pltpu.VMEM((2048, 512), BF16),
            pltpu.VMEM((256, 2048), BF16),
            pltpu.VMEM((2, 2048, 512), BF16),
            pltpu.VMEM((32, 2, 2, 128, 128), BF16),
            pltpu.VMEM((32, 2, 16, 512), BF16),
            pltpu.VMEM((GROUPS, 4, 128, 128), BF16),
            pltpu.VMEM((8192, 128), BF16),
            pltpu.VMEM((8192, 256), BF16),
            pltpu.VMEM((1024, 2048), BF16),
            pltpu.VMEM((2, 128, 2048), BF16),
            pltpu.VMEM((32, 2, 16, 512), BF16),
            pltpu.VMEM((1024, 512), BF16),
            pltpu.VMEM((256, 2048), F32),
            pltpu.VMEM((128, 2048), F32),
            pltpu.VMEM((128, 2048), F32),
            pltpu.VMEM((128, 2048), BF16),
            pltpu.VMEM((128, 2048), BF16),
            pltpu.VMEM((1024, 512), BF16),
            pltpu.VMEM((64, 16, 512), BF16),
            pltpu.VMEM((32, 2, 16, 512), BF16),
            pltpu.VMEM((2, 128, 2048), BF16),
            pltpu.VMEM((32, 64, 512), BF16),
            pltpu.VMEM((8, 64, 2048), BF16),
            pltpu.VMEM((M, CW), F32),
            pltpu.VMEM((M, CW), F32),
            pltpu.VMEM((M, 128), F32),
            pltpu.VMEM((M, 256), F32),
            dma((6,)), dma((2,)),
            dma((4, 2)), dma((4, 2)),
            dma((4,)), dma((4,)), dma((4,)), dma((4,)),
            dma((N,)), dma((N,)), dma((3,)), dma((3,)), dma((N,)), dma((N,)),
            dma((GROUPS, 4)), dma((GROUPS, 4)),
            dma((N,)), dma((N,)), dma((N,)), dma((N,)),
        ],
        compiler_params=pltpu.CompilerParams(
            collective_id=0, has_side_effects=True, vmem_limit_bytes=60 * 1024 * 1024
        ),
    )(
        query_states[0].reshape(2, 128, 2048), key_states[0].reshape(2, 128, 512), value_states[0].reshape(2, 128, 512),
        layer_inputs[0].reshape(2, 128, 2048), out_weight[0], teacher, teacher_map, order,
    )
    return sh.reshape(1, 256, 2048), wg[None]


def solution(mesh):
    return jax.shard_map(
        local,
        mesh=mesh,
        in_specs=(
            P("student", "ctx", None),
            P("student", "ctx", None),
            P("student", "ctx", None),
            P("student", "ctx", None),
            P("student", None, None),
            P("ctx", "student"),
            P("student", None),
            P(),
        ),
        out_specs=(P("student", "ctx", None), P("student", "ctx", None)),
        check_vma=False,
    )
```

time: 843 us -> 145 us (0.17)
  waiting for transfers between devices: 417 us -> 0 us
  matrix products: 258 us -> 0 us
  Pallas kernels: 0 us -> 137 us
  other arithmetic: 88.7 us -> 1.45 us
  local copies, waits for them, and re-layouts: 61.2 us -> 4.18 us
  between operations: 15.3 us -> 0.66 us
    dot_general x35 -> x0, matrix products: 258 us -> none  [the longest x16 161 us: one_block(): jnp.einsum('hgqk,khd->hgqd', expo, value_block.astype(jnp.float32), preci...]
    reduce_scatter x1 -> x0, waiting for transfers between devices: 222 us -> none  [local(): lax.psum_scatter(lax.dot_general(attended, match_grad, (((0,), (0,)), (()...]
    all_gather x2 -> x0, waiting for transfers between devices: 194 us -> none  [the longest x1 102 us: attention(): key_piece = lax.all_gather(key_local, 'ctx', axis=0, tiled=True)]
    pallas_call x0 -> x1, Pallas kernels: none -> 137 us  [local(): pl.pallas_call(kernel, name='layer', out_shape=(jax.ShapeDtypeStruct((2,...]
    reduce_sum x18 -> x1, other arithmetic: 84.5 us -> 0.11 us  [local(): jnp.sum(jnp.where(pos[None, :] == ids[:, None], ids[None, :], 0), axis=1)]
    dynamic_slice x32 -> x0, local copies, waits for them, and re-layouts: 25.2 us -> none  [attention(): result, _ = lax.scan(one_block, init, (key_blocks, value_blocks, key_pos))]
    reshape x2 -> x0, local copies, waits for them, and re-layouts: 25.1 us -> none  [the longest x1 12.6 us: attention(): key_blocks = key_piece.reshape(number, width, HK, HD)]
    while x49 -> x0, local copies, waits for them, and re-layouts: 9.66 us -> none
  transfers between devices with their start and end apart: 4 -> 0, of which waited for: 3 -> 0; matrix products, arithmetic and copies ran while one was open for 46% -> 0% of each run, Pallas kernels for 0% -> 0%
where the time goes in v1:
time: 145 us; the launch traced here: 143 us
  Pallas kernels  137 us (94%)
  local copies, waits for them, and re-layouts  4.18 us (3%)
  other arithmetic  1.45 us (1%)
    pallas_call x1, Pallas kernels, local(): pl.pallas_call(kernel, name='layer', out_shape=(jax.ShapeDtypeStruct((2,...  137 us
    unnamed x2, local copies, waits for them, and re-layouts  4.18 us

profile of v1, /device:TPU:2, one launch (start us, length us, event | category | flops | bytes accessed | tf_op | source)
XLA Modules:
  0.0 143.1 jit_solution(704361297750571428)
XLA Ops:
  0.6 0.7 and_select_fusion.6
  1.3 0.1 select_reduce_fusion
  1.5 0.6 pad_add_fusion.order
  2.1 136.9 %layer.1 = (bf16[2,128,2048]{2,1,0:T(8,128)(2,1)}, f32[64,2048]{1,0:T(8,128)}) custom-call(bf16[2,128,2048]{2,1,0:T(8,128)(2,1)} %bitcast.8, bf16[2,128,512]{2,1,0:T(8,128)(2,1)} %bitcast.12, bf16[2,128,512]{2,1,0:T(8,128)(2,1)} %bitcast.13, bf16[2,128,2048]{2,1,0:T(8,128)(2,1)} %bitcast.9, bf16[2048,2048]{1,0:T(8,128)(2,1)} %bitcast.7, ...), custom_call_target="tpu_custom_call" | custom-call | tf_op jit(solution)/shard_map/layer/pallas_call | solution.py:402
  139.0 2.3 %copy.12 = bf16[1,256,2048]{2,1,0:T(8,128)(2,1)} copy(bf16[1,256,2048]{2,1,0:T(8,128)(2,1)} %bitcast.10) | data formatting | bytes 2097152
  141.3 1.9 %copy.13 = f32[1,64,2048]{2,1,0:T(8,128)} copy(f32[1,64,2048]{2,1,0:T(8,128)} %bitcast.11) | data formatting | bytes 1048576
  (1 shorter events, 0.0 us)

commit v2 on v1

--- a/solution.py
+++ b/solution.py
@@ -22,12 +22,12 @@
 
 def kernel(
     q, k, v, li, w, te, tm, order,
-    sh_out, wg_out,
+    sh_recv, wg_out_v,
     li_v, w_v, te_v, tm_v, kv, q_recv, qp, kpos, vp, att, d_home, d_recv, dpos,
-    tp, tx, tt, th, th_recv, mg, aw, sh_send, sh_recv, wg_send, wg_recv,
+    tp, tx, tt, th, th_recv, mg, aw, sh_send, wg_send, wa_recv, wb_send,
     sa, sb, m_ref, acc,
-    loc, loc_tm, s1_s, s1_r, g_s, g_r, x_s, x_r, q_s, q_r, t_s, t_r, d_s, d_r,
-    ag_s, ag_r, sh_s, sh_r, wg_s, wg_r,
+    loc, loc_tm, s1_s, s1_r, g_s, g_r, q_s, q_r, t_s, t_r, d_s, d_r,
+    ag_s, ag_r, sh_s, sh_r, wa_s, wa_r, wb_s, wb_r,
 ):
     stu = lax.axis_index("student")
     me = lax.axis_index("ctx")
@@ -116,15 +116,29 @@
         for i in range(2):
             at = kv.at[xh * 16 + b * 4 + frm, i]
             remote(at, at, s1_s.at[da, i], s1_r.at[da, i], {"ctx": ctx_of(xh, frm, b)}).wait_recv()
-    own = kv.at[pl.ds(xh * 16 + b * 4, 4)]
-    other = kv.at[pl.ds((1 - xh) * 16 + b * 4, 4)]
-    seconds = [remote(own, own, g_s.at[0], g_r.at[0], {"ctx": ctx_of(1 - xh, a, b)})]
-    for db in range(1, 4):
-        seconds.append(
-            remote(own, own, g_s.at[db], g_r.at[db], {"ctx": ctx_of(xh, a, lax.rem(b + db, 4))})
-        )
-    for c in seconds:
+    right, left, across = lax.rem(b + 1, 4), lax.rem(b + 3, 4), lax.rem(b + 2, 4)
+
+    def kv_rows(x_, b_, first, count):
+        return kv.at[pl.ds(x_ * 16 + b_ * 4 + first, count)]
+
+    def kv_copy(n, x_from, b_from, first, count, x_to, b_to):
+        at = kv_rows(x_from, b_from, first, count)
+        return remote(at, at, g_s.at[n], g_r.at[n], {"ctx": ctx_of(x_to, a, b_to)})
+
+    xo = 1 - xh
+    sent = []
+
+    def send(*args):
+        c = kv_copy(*args)
         c.start()
+        sent.append(c)
+
+    def arrive(*args):
+        kv_copy(*args).wait_recv()
+
+    send(0, xh, b, 0, 4, xo, b)
+    send(1, xh, b, 0, 4, xh, right)
+    send(2, xh, b, 0, 4, xh, left)
 
     vp[:, HD:] = jnp.ones((8192, HD), BF16)
     c_te.wait()
@@ -142,14 +156,13 @@
     t2 = remote(th, th_recv, t_s.at[1], t_r.at[1], pair_xlo)
     t2.start()
 
-    remote(other, other, g_s.at[0], g_r.at[0], {"ctx": ctx_of(1 - xh, a, b)}).wait_recv()
-    thirds = []
-    for db in range(1, 4):
-        thirds.append(
-            remote(other, other, x_s.at[db], x_r.at[db], {"ctx": ctx_of(xh, a, lax.rem(b + db, 4))})
-        )
-    for c in thirds:
-        c.start()
+    arrive(0, xo, b, 0, 4, xo, b)
+    send(3, xo, b, 0, 4, xh, right)
+    send(4, xo, b, 0, 4, xh, left)
+    arrive(1, xh, left, 0, 4, xh, left)
+    send(5, xh, left, 0, 2, xh, right)
+    arrive(2, xh, right, 0, 4, xh, right)
+    send(6, xh, right, 2, 2, xh, left)
     t2.wait()
     tp[half, :] = tp[half, :] + tx[...] + th_recv[...].astype(F32)
     t3 = remote(tp.at[half], tt, t_s.at[2], t_r.at[2], pair_core)
@@ -159,6 +172,10 @@
     t3.wait()
     d_home[1 - core] = (li_v[1 - core].astype(F32) - tt[...]).astype(BF16)
 
+    arrive(3, xo, left, 0, 4, xh, left)
+    send(7, xo, left, 0, 2, xh, right)
+    arrive(4, xo, right, 0, 4, xh, right)
+    send(8, xo, right, 2, 2, xh, left)
     c_q.wait()
 
     def q_wait(kk, _):
@@ -168,12 +185,10 @@
         return 0
 
     lax.fori_loop(1, N, q_wait, 0)
-    for db in range(1, 4):
-        frm = lax.rem(b - db + 4, 4)
-        at = kv.at[pl.ds(xh * 16 + frm * 4, 4)]
-        remote(at, at, g_s.at[db], g_r.at[db], {"ctx": ctx_of(xh, a, frm)}).wait_recv()
-        at = kv.at[pl.ds((1 - xh) * 16 + frm * 4, 4)]
-        remote(at, at, x_s.at[db], x_r.at[db], {"ctx": ctx_of(xh, a, frm)}).wait_recv()
+    arrive(5, xh, across, 0, 2, xh, left)
+    arrive(6, xh, across, 2, 2, xh, right)
+    arrive(7, xo, across, 0, 2, xh, left)
+    arrive(8, xo, across, 2, 2, xh, right)
 
     def d_copy(kk):
         x_, a_, b_ = peer(kk, 1)
@@ -323,28 +338,56 @@
     lax.fori_loop(1, N, sh_start, 0)
     sh_recv[:, cols(t, 16), cols(a, 512)] = sh_send[me]
 
-    def wg_copy(to):
+    def wgrad(i, _):
+        part = lax.dot_general(
+            att[:, cols(i, 256)], mg[...], (((0,), (0,)), ((), ())), preferred_element_type=F32
+        ).astype(BF16)
+        for r in range(4):
+            x_, mid_, low_ = i // 4, lax.rem(i, 4), r
+            a_ = jnp.where(core == 0, low_, mid_)
+            b_ = jnp.where(core == 0, mid_, low_)
+            wg_send[x_, b_, a_] = part[r * 64 : r * 64 + 64]
+        return 0
+
+    lax.fori_loop(0, 8, wgrad, 0)
+
+    def wa_copy(x_, db):
+        to = lax.rem(b + db, 4)
         return remote(
-            wg_send.at[to], wg_recv.at[t, :, cols(a, 512)], wg_s.at[to], wg_r.at[me], {"ctx": to}
-        )
-
-    def wgrad(i, _):
-        quad = lax.rem(me // 4 + i, 8)
-        part = lax.dot_general(
-            att[:, cols(quad, 256)], mg[...], (((0,), (0,)), ((), ())), preferred_element_type=F32
-        ).astype(BF16)
-        wg_send[pl.ds(quad * 4, 4)] = part.reshape(4, 64, 512)
-        for r in range(4):
-            to = quad * 4 + r
-
-            @pl.when(to != me)
-            def _():
-                wg_copy(to).start()
-
-        return 0
-
-    lax.fori_loop(0, 8, wgrad, 0)
-    wg_recv[t, :, cols(a, 512)] = wg_send[me]
+            wg_send.at[x_, to], wa_recv.at[x_, db - 1], wa_s.at[x_, db], wa_r.at[x_, db],
+            {"ctx": ctx_of(xh, a, to)},
+        )
+
+    for x_ in (xo, xh):
+        for db in range(1, 4):
+            wa_copy(x_, db).start()
+
+    def wb_copy(da, far):
+        to = lax.rem(a + da, 4)
+        x_ = xo if far else xh
+        return remote(
+            wb_send.at[x_, to], wg_out_v.at[xh, :, cols(a, 512)], wb_s.at[far, da], wb_r.at[far, da],
+            {"ctx": ctx_of(x_, to, b)},
+        )
+
+    for far in (1, 0):
+        x_ = xo if far else xh
+        for db in range(1, 4):
+            frm = lax.rem(b - db + 4, 4)
+            remote(
+                wg_send.at[x_, frm], wa_recv.at[x_, db - 1], wa_s.at[x_, db], wa_r.at[x_, db],
+                {"ctx": ctx_of(xh, a, frm)},
+            ).wait_recv()
+        for da in range(4):
+            to = lax.rem(a + da, 4)
+            total = wg_send[x_, b, to].astype(F32)
+            for db in range(1, 4):
+                total = total + wa_recv[x_, db - 1, to].astype(F32)
+            if far == 0 and da == 0:
+                wg_out_v[xh, :, cols(a, 512)] = total.astype(BF16)
+            else:
+                wb_send[x_, to] = total.astype(BF16)
+                wb_copy(da, far).start()
 
     def sh_wait(kk, _):
         x_, a_, b_ = peer(kk, -1)
@@ -353,29 +396,24 @@
         return 0
 
     lax.fori_loop(1, N, sh_wait, 0)
-    sh_out[...] = (li_v[...].astype(F32) + sh_recv[...].astype(F32)).astype(BF16)
-
-    def wg_wait(kk, _):
-        x_, a_, b_ = peer(kk, -1)
-        frm = ctx_of(x_, a_, b_)
-        at = wg_recv.at[x_ * 4 + b_, :, cols(a_, 512)]
-        remote(wg_send.at[0], at, wg_s.at[frm], wg_r.at[frm], {"ctx": frm}).wait_recv()
-        return 0
-
-    lax.fori_loop(1, N, wg_wait, 0)
-    total = wg_recv[0].astype(F32)
-    for i in range(1, 8):
-        total = total + wg_recv[i].astype(F32)
-    wg_out[...] = total
-
-    for c in firsts + seconds + thirds:
+    for far in (1, 0):
+        x_ = xo if far else xh
+        for da in range(4):
+            if far == 0 and da == 0:
+                continue
+            frm = lax.rem(a - da + 4, 4)
+            remote(
+                wb_send.at[x_, frm], wg_out_v.at[x_, :, cols(frm, 512)], wb_s.at[far, da], wb_r.at[far, da],
+                {"ctx": ctx_of(x_, frm, b)},
+            ).wait_recv()
+
+    for c in firsts + sent:
         c.wait_send()
 
     def drain(kk, _):
         q_copy(kk).wait_send()
         d_copy(kk).wait_send()
         sh_copy(kk).wait_send()
-        wg_copy(lax.rem(me + kk, N)).wait_send()
         return 0
 
     lax.fori_loop(1, N, drain, 0)
@@ -386,6 +424,13 @@
         return 0
 
     lax.fori_loop(0, GROUPS, drain_att, 0)
+    for x_ in (xo, xh):
+        for db in range(1, 4):
+            wa_copy(x_, db).wait_send()
+    for far in (1, 0):
+        for da in range(4):
+            if far or da:
+                wb_copy(da, far).wait_send()
 
 
 def local(query_states, key_states, value_states, layer_inputs, out_weight, teacher, teacher_map, offsets):
@@ -404,7 +449,7 @@
         name="layer",
         out_shape=(
             jax.ShapeDtypeStruct((2, 128, 2048), BF16),
-            jax.ShapeDtypeStruct((64, 2048), F32),
+            jax.ShapeDtypeStruct((2, 64, 2048), BF16),
         ),
         in_specs=[hbm] * 7 + [pl.BlockSpec(memory_space=pltpu.SMEM)],
         out_specs=(vmem, vmem),
@@ -430,19 +475,19 @@
             pltpu.VMEM((1024, 512), BF16),
             pltpu.VMEM((64, 16, 512), BF16),
             pltpu.VMEM((32, 2, 16, 512), BF16),
-            pltpu.VMEM((2, 128, 2048), BF16),
-            pltpu.VMEM((32, 64, 512), BF16),
-            pltpu.VMEM((8, 64, 2048), BF16),
+            pltpu.VMEM((2, 4, 4, 64, 512), BF16),
+            pltpu.VMEM((2, 3, 4, 64, 512), BF16),
+            pltpu.VMEM((2, 4, 64, 512), BF16),
             pltpu.VMEM((M, CW), F32),
             pltpu.VMEM((M, CW), F32),
             pltpu.VMEM((M, 128), F32),
             pltpu.VMEM((M, 256), F32),
             dma((6,)), dma((2,)),
             dma((4, 2)), dma((4, 2)),
-            dma((4,)), dma((4,)), dma((4,)), dma((4,)),
+            dma((9,)), dma((9,)),
             dma((N,)), dma((N,)), dma((3,)), dma((3,)), dma((N,)), dma((N,)),
             dma((GROUPS, 4)), dma((GROUPS, 4)),
-            dma((N,)), dma((N,)), dma((N,)), dma((N,)),
+            dma((N,)), dma((N,)), dma((2, 4)), dma((2, 4)), dma((2, 4)), dma((2, 4)),
         ],
         compiler_params=pltpu.CompilerParams(
             collective_id=0, has_side_effects=True, vmem_limit_bytes=60 * 1024 * 1024
@@ -451,7 +496,8 @@
         query_states[0].reshape(2, 128, 2048), key_states[0].reshape(2, 128, 512), value_states[0].reshape(2, 128, 512),
         layer_inputs[0].reshape(2, 128, 2048), out_weight[0], teacher, teacher_map, order,
     )
-    return sh.reshape(1, 256, 2048), wg[None]
+    hidden = (layer_inputs[0].astype(F32) + sh.reshape(256, 2048).astype(F32)).astype(BF16)
+    return hidden[None], (wg[0].astype(F32) + wg[1].astype(F32))[None]
 
 
 def solution(mesh):

time: 145 us -> 142 us (0.979)
  local copies, waits for them, and re-layouts: 4.18 us -> 0.01 us
  other arithmetic: 1.45 us -> 4.94 us
  Pallas kernels: 137 us -> 135 us
    unnamed x2 -> x4, local copies, waits for them, and re-layouts: 4.18 us -> 0.01 us
    convert_element_type x0 -> x1, other arithmetic: none -> 2.65 us  [local(): (layer_inputs[0].astype(F32) + sh.reshape(256, 2048).astype(F32)).astype(...]
    pallas_call x1, Pallas kernels: 137 us -> 135 us  [local(): pl.pallas_call(kernel, name='layer', out_shape=(jax.ShapeDtypeStruct((2,...]
where the time goes in v2:
time: 142 us; the launch traced here: 140 us
  Pallas kernels  135 us (95%)
  other arithmetic  4.94 us (3%)
    pallas_call x1, Pallas kernels, local(): pl.pallas_call(kernel, name='layer', out_shape=(jax.ShapeDtypeStruct((2,...  135 us

profile of v2, /device:TPU:2, one launch (start us, length us, event | category | flops | bytes accessed | tf_op | source)
XLA Modules:
  0.0 140.2 jit_solution(9369074195769330096)
XLA Ops:
  0.6 0.7 and_select_fusion.6
  1.3 0.1 select_reduce_fusion
  1.5 0.6 pad_add_fusion.order
  2.1 0.0 copy-start
  2.1 134.5 %layer.1 = (bf16[2,128,2048]{2,1,0:T(8,128)(2,1)}, bf16[2,64,2048]{2,1,0:T(8,128)(2,1)}) custom-call(bf16[2,128,2048]{2,1,0:T(8,128)(2,1)} %bitcast.11, bf16[2,128,512]{2,1,0:T(8,128)(2,1)} %bitcast.13, bf16[2,128,512]{2,1,0:T(8,128)(2,1)} %bitcast.14, bf16[2,128,2048]{2,1,0:T(8,128)(2,1)} %bitcast.10, bf16[2048,2048]{1,0:T(8,128)(2,1)} %bitcast.9, ...), custom_call_target="tpu_custom_call" | custom-call | tf_op jit(solution)/shard_map/layer/pallas_call | solution.py:447
  136.7 0.0 copy-start.1
  136.7 0.0 copy-done
  136.7 2.6 %fusion = bf16[1,256,2048]{2,1,0:T(8,128)(2,1)} fusion(bf16[1,256,2048]{2,1,0:T(8,128)(2,1)S(1)} %copy-done, bf16[1,256,2048]{2,1,0:T(8,128)(2,1)} %bitcast.12), kind=kLoop, calls=%fused_computation.1 | loop fusion | flops 2097152 | bytes 3145728 | tf_op jit(solution)/shard_map/convert_element_type | solution.py:499
  139.3 0.0 copy-done.1
  139.3 0.8 convert_add_fusion.1
  (1 shorter events, 0.0 us)
Async XLA Ops:
  2.1 134.6 %copy-start = (bf16[1,256,2048]{2,1,0:T(8,128)(2,1)S(1)}, bf16[1,256,2048]{2,1,0:T(8,128)(2,1)}, u32[]{:S(2)}) copy-start(bf16[1,256,2048]{2,1,0:T(8,128)(2,1)} %param.11) | copy-start | bytes 3145732
  136.7 2.7 %copy-start.1 = (bf16[2,64,2048]{2,1,0:T(8,128)(2,1)S(1)}, bf16[2,64,2048]{2,1,0:T(8,128)(2,1)}, u32[]{:S(2)}) copy-start(bf16[2,64,2048]{2,1,0:T(8,128)(2,1)} %get-tuple-element.5) | copy-start | bytes 1572868

commit v3 on v2

--- a/solution.py
+++ b/solution.py
@@ -84,18 +84,49 @@
     pl.semaphore_signal(barrier, inc=1, device_id=pair_xlo, device_id_type=MESH)
     pl.semaphore_wait(barrier, N + 1)
 
-    firsts = []
-    for da in range(1, 4):
+    xo = 1 - xh
+    right, left, across = lax.rem(b + 1, 4), lax.rem(b + 3, 4), lax.rem(b + 2, 4)
+    sent = []
+
+    def first_copy(far, da, i):
         to = lax.rem(a + da, 4)
-        for i, src in enumerate((k, v)):
-            firsts.append(
-                remote(
-                    src.at[:, :, cols(to, HD)], kv.at[mine, i], s1_s.at[da, i], s1_r.at[da, i],
-                    {"ctx": ctx_of(xh, to, b)},
-                )
-            )
-    for c in firsts:
+        return remote(
+            (k, v)[i].at[:, :, cols(to, HD)], kv.at[mine, i], s1_s.at[far, da, i], s1_r.at[far, da, i],
+            {"ctx": ctx_of(xo if far else xh, to, b)},
+        )
+
+    for far, da in ((0, 1), (1, 0), (0, 2), (1, 1), (0, 3), (1, 2), (1, 3)):
+        for i in range(2):
+            c = first_copy(far, da, i)
+            c.start()
+            sent.append(c)
+
+    def piece(far, r, b_):
+        return kv.at[(xo if far else xh) * 16 + b_ * 4 + lax.rem(a - r + 4, 4)]
+
+    def hop(far, r, way, b_):
+        at = piece(far, r, b_)
+        return remote(
+            at, at, g_s.at[far, r, way], g_r.at[far, r, way], {"ctx": ctx_of(xh, a, left if way % 2 else right)}
+        )
+
+    def pass_on(far, r):
+        for i in range(2):
+            if far or r:
+                at = piece(far, r, b).at[i]
+                remote(at, at, s1_s.at[far, r, i], s1_r.at[far, r, i], {"ctx": ctx_of(xh, a, right)}).wait_recv()
+        for way in range(2):
+            c = hop(far, r, way, b)
+            c.start()
+            sent.append(c)
+
+    def relay(far, r):
+        way = r % 2
+        frm = right if way else left
+        hop(far, r, way, frm).wait_recv()
+        c = hop(far, r, 2 + way, frm)
         c.start()
+        sent.append(c)
 
     def q_copy(kk, sign=1):
         x_, a_, b_ = peer(kk, sign)
@@ -108,74 +139,40 @@
         q_copy(kk).start()
         return 0
 
-    lax.fori_loop(1, N, q_start, 0)
     c_k.wait()
     c_v.wait()
-    for da in range(1, 4):
-        frm = lax.rem(a - da + 4, 4)
-        for i in range(2):
-            at = kv.at[xh * 16 + b * 4 + frm, i]
-            remote(at, at, s1_s.at[da, i], s1_r.at[da, i], {"ctx": ctx_of(xh, frm, b)}).wait_recv()
-    right, left, across = lax.rem(b + 1, 4), lax.rem(b + 3, 4), lax.rem(b + 2, 4)
-
-    def kv_rows(x_, b_, first, count):
-        return kv.at[pl.ds(x_ * 16 + b_ * 4 + first, count)]
-
-    def kv_copy(n, x_from, b_from, first, count, x_to, b_to):
-        at = kv_rows(x_from, b_from, first, count)
-        return remote(at, at, g_s.at[n], g_r.at[n], {"ctx": ctx_of(x_to, a, b_to)})
-
-    xo = 1 - xh
-    sent = []
-
-    def send(*args):
-        c = kv_copy(*args)
-        c.start()
-        sent.append(c)
-
-    def arrive(*args):
-        kv_copy(*args).wait_recv()
-
-    send(0, xh, b, 0, 4, xo, b)
-    send(1, xh, b, 0, 4, xh, right)
-    send(2, xh, b, 0, 4, xh, left)
-
+    pass_on(0, 0)
+    lax.fori_loop(1, N, q_start, 0)
     vp[:, HD:] = jnp.ones((8192, HD), BF16)
+    for r in range(1, 4):
+        pass_on(0, r)
     c_te.wait()
     for i in range(4):
         tm_loads[i].wait()
         tp[:, 512 * i : 512 * i + 512] = jnp.dot(te_v[...], tm_v[i % 2], preferred_element_type=F32)
         if i < 2:
             tm_loads[i + 2].start()
+        pass_on(1, i)
     half = pl.ds(pl.multiple_of(core * 128, 128), 128)
     half2 = pl.ds(pl.multiple_of((1 - core) * 128, 128), 128)
     t1 = remote(tp.at[half2], tx, t_s.at[0], t_r.at[0], pair_core)
     t1.start()
+    for r in range(4):
+        relay(0, r)
     t1.wait()
-    th[...] = (tp[half, :] + tx[...]).astype(BF16)
+    tp[half, :] = tp[half, :] + tx[...]
+    th[...] = tp[half, :].astype(BF16)
     t2 = remote(th, th_recv, t_s.at[1], t_r.at[1], pair_xlo)
     t2.start()
-
-    arrive(0, xo, b, 0, 4, xo, b)
-    send(3, xo, b, 0, 4, xh, right)
-    send(4, xo, b, 0, 4, xh, left)
-    arrive(1, xh, left, 0, 4, xh, left)
-    send(5, xh, left, 0, 2, xh, right)
-    arrive(2, xh, right, 0, 4, xh, right)
-    send(6, xh, right, 2, 2, xh, left)
+    for r in range(4):
+        relay(1, r)
     t2.wait()
-    tp[half, :] = tp[half, :] + tx[...] + th_recv[...].astype(F32)
+    tp[half, :] = tp[half, :] + th_recv[...].astype(F32)
     t3 = remote(tp.at[half], tt, t_s.at[2], t_r.at[2], pair_core)
     t3.start()
     c_li.wait()
     d_home[core] = (li_v[core].astype(F32) - tp[half, :]).astype(BF16)
-    t3.wait()
-    d_home[1 - core] = (li_v[1 - core].astype(F32) - tt[...]).astype(BF16)
-
-    arrive(3, xo, left, 0, 4, xh, left)
-    send(7, xo, left, 0, 2, xh, right)
-    arrive(4, xo, right, 0, 4, xh, right)
-    send(8, xo, right, 2, 2, xh, left)
+
     c_q.wait()
 
     def q_wait(kk, _):
@@ -185,10 +182,13 @@
         return 0
 
     lax.fori_loop(1, N, q_wait, 0)
-    arrive(5, xh, across, 0, 2, xh, left)
-    arrive(6, xh, across, 2, 2, xh, right)
-    arrive(7, xo, across, 0, 2, xh, left)
-    arrive(8, xo, across, 2, 2, xh, right)
+    for far in range(2):
+        for r in range(4):
+            way = 1 - r % 2
+            hop(far, r, way, right if way else left).wait_recv()
+            hop(far, r, 2 + r % 2, across).wait_recv()
+    t3.wait()
+    d_home[1 - core] = (li_v[1 - core].astype(F32) - tt[...]).astype(BF16)
 
     def d_copy(kk):
         x_, a_, b_ = peer(kk, 1)
@@ -407,7 +407,7 @@
                 {"ctx": ctx_of(x_, frm, b)},
             ).wait_recv()
 
-    for c in firsts + sent:
+    for c in sent:
         c.wait_send()
 
     def drain(kk, _):
@@ -483,8 +483,8 @@
             pltpu.VMEM((M, 128), F32),
             pltpu.VMEM((M, 256), F32),
             dma((6,)), dma((2,)),
-            dma((4, 2)), dma((4, 2)),
-            dma((9,)), dma((9,)),
+            dma((2, 4, 2)), dma((2, 4, 2)),
+            dma((2, 4, 4)), dma((2, 4, 4)),
             dma((N,)), dma((N,)), dma((3,)), dma((3,)), dma((N,)), dma((N,)),
             dma((GROUPS, 4)), dma((GROUPS, 4)),
             dma((N,)), dma((N,)), dma((2, 4)), dma((2, 4)), dma((2, 4)), dma((2, 4)),

time: 142 us -> 130 us (0.915)
  Pallas kernels: 135 us -> 124 us
    pallas_call x1, Pallas kernels: 135 us -> 124 us  [local(): pl.pallas_call(kernel, name='layer', out_shape=(jax.ShapeDtypeStruct((2,...]
where the time goes in v3:
time: 130 us
  Pallas kernels  124 us (95%)
  other arithmetic  4.94 us (4%)
    pallas_call x1, Pallas kernels, local(): pl.pallas_call(kernel, name='layer', out_shape=(jax.ShapeDtypeStruct((2,...  124 us
    convert_element_type x1, other arithmetic, local(): (layer_inputs[0].astype(F32) + sh.reshape(256, 2048).astype(F32)).astype(...  2.65 us

profile of v3, /device:TPU:2, one launch (start us, length us, event | category | flops | bytes accessed | tf_op | source)
XLA Modules:
  0.0 129.5 jit_solution(3200077657594461158)
XLA Ops:
  0.6 0.7 and_select_fusion.6
  1.3 0.1 select_reduce_fusion
  1.5 0.6 pad_add_fusion.order
  2.1 0.0 copy-start
  2.1 123.9 %layer.1 = (bf16[2,128,2048]{2,1,0:T(8,128)(2,1)}, bf16[2,64,2048]{2,1,0:T(8,128)(2,1)}) custom-call(bf16[2,128,2048]{2,1,0:T(8,128)(2,1)} %bitcast.11, bf16[2,128,512]{2,1,0:T(8,128)(2,1)} %bitcast.13, bf16[2,128,512]{2,1,0:T(8,128)(2,1)} %bitcast.14, bf16[2,128,2048]{2,1,0:T(8,128)(2,1)} %bitcast.10, bf16[2048,2048]{1,0:T(8,128)(2,1)} %bitcast.9, ...), custom_call_target="tpu_custom_call" | custom-call | tf_op jit(solution)/shard_map/layer/pallas_call | solution.py:447
  126.0 0.0 copy-start.1
  126.0 0.0 copy-done
  126.1 2.6 %fusion = bf16[1,256,2048]{2,1,0:T(8,128)(2,1)} fusion(bf16[1,256,2048]{2,1,0:T(8,128)(2,1)S(1)} %copy-done, bf16[1,256,2048]{2,1,0:T(8,128)(2,1)} %bitcast.12), kind=kLoop, calls=%fused_computation.1 | loop fusion | flops 2097152 | bytes 3145728 | tf_op jit(solution)/shard_map/convert_element_type | solution.py:499
  128.7 0.0 copy-done.1
  128.7 0.8 convert_add_fusion.1
  (1 shorter events, 0.0 us)
Async XLA Ops:
  2.1 123.9 %copy-start = (bf16[1,256,2048]{2,1,0:T(8,128)(2,1)S(1)}, bf16[1,256,2048]{2,1,0:T(8,128)(2,1)}, u32[]{:S(2)}) copy-start(bf16[1,256,2048]{2,1,0:T(8,128)(2,1)} %param.11) | copy-start | bytes 3145732
  126.0 2.7 %copy-start.1 = (bf16[2,64,2048]{2,1,0:T(8,128)(2,1)S(1)}, bf16[2,64,2048]{2,1,0:T(8,128)(2,1)}, u32[]{:S(2)}) copy-start(bf16[2,64,2048]{2,1,0:T(8,128)(2,1)} %get-tuple-element.5) | copy-start | bytes 1572868

commit v4 on v3

--- a/solution.py
+++ b/solution.py
@@ -21,11 +21,11 @@
 
 
 def kernel(
-    q, k, v, li, w, te, tm, order,
+    q, k, v, li, w, te, tm, pos, where,
     sh_recv, wg_out_v,
     li_v, w_v, te_v, tm_v, kv, q_recv, qp, kpos, vp, att, d_home, d_recv, dpos,
     tp, tx, tt, th, th_recv, mg, aw, sh_send, wg_send, wa_recv, wb_send,
-    sa, sb, m_ref, acc,
+    sa, sb, ma, mb, m_ref, acc,
     loc, loc_tm, s1_s, s1_r, g_s, g_r, q_s, q_r, t_s, t_r, d_s, d_r,
     ag_s, ag_r, sh_s, sh_r, wa_s, wa_r, wb_s, wb_r,
 ):
@@ -43,9 +43,9 @@
     def ctx_of(x_, a_, b_):
         return x_ * 16 + jnp.where(core == 0, b_ * 4 + a_, a_ * 4 + b_)
 
-    def remote(src, dst, ss, rs, where):
+    def remote(src, dst, ss, rs, target):
         return pltpu.make_async_remote_copy(
-            src_ref=src, dst_ref=dst, send_sem=ss, recv_sem=rs, device_id=where, device_id_type=MESH
+            src_ref=src, dst_ref=dst, send_sem=ss, recv_sem=rs, device_id=target, device_id_type=MESH
         )
 
     def cols(i, width):
@@ -65,9 +65,9 @@
     c_te = pltpu.make_async_copy(te, te_v, loc.at[0])
     c_li = pltpu.make_async_copy(li, li_v, loc.at[1])
     c_w = pltpu.make_async_copy(w.at[:, cols(a, 512)], w_v, loc.at[2])
-    c_k = pltpu.make_async_copy(k.at[:, :, cols(a, HD)], kv.at[mine, 0], loc.at[3])
-    c_v = pltpu.make_async_copy(v.at[:, :, cols(a, HD)], kv.at[mine, 1], loc.at[4])
-    c_q = pltpu.make_async_copy(q.at[:, cols(t, 16), cols(a, 512)], q_recv.at[mine], loc.at[5])
+    c_k = pltpu.make_async_copy(k.at[:, :, cols(a, HD)], kv.at[pl.ds(2 * mine, 2), 0], loc.at[3])
+    c_v = pltpu.make_async_copy(v.at[:, :, cols(a, HD)], kv.at[pl.ds(2 * mine, 2), 1], loc.at[4])
+    c_q = pltpu.make_async_copy(q.at[:, cols(t, 16), cols(a, 512)], q_recv.at[pl.ds(2 * mine, 2)], loc.at[5])
     for c in (c_k, c_v, c_q, c_te, tm_loads[0], tm_loads[1], c_li, c_w):
         c.start()
 
@@ -91,7 +91,7 @@
     def first_copy(far, da, i):
         to = lax.rem(a + da, 4)
         return remote(
-            (k, v)[i].at[:, :, cols(to, HD)], kv.at[mine, i], s1_s.at[far, da, i], s1_r.at[far, da, i],
+            (k, v)[i].at[:, :, cols(to, HD)], kv.at[pl.ds(2 * mine, 2), i], s1_s.at[far, da, i], s1_r.at[far, da, i],
             {"ctx": ctx_of(xo if far else xh, to, b)},
         )
 
@@ -102,7 +102,7 @@
             sent.append(c)
 
     def piece(far, r, b_):
-        return kv.at[(xo if far else xh) * 16 + b_ * 4 + lax.rem(a - r + 4, 4)]
+        return kv.at[pl.ds(2 * ((xo if far else xh) * 16 + b_ * 4 + lax.rem(a - r + 4, 4)), 2)]
 
     def hop(far, r, way, b_):
         at = piece(far, r, b_)
@@ -113,7 +113,7 @@
     def pass_on(far, r):
         for i in range(2):
             if far or r:
-                at = piece(far, r, b).at[i]
+                at = piece(far, r, b).at[:, i]
                 remote(at, at, s1_s.at[far, r, i], s1_r.at[far, r, i], {"ctx": ctx_of(xh, a, right)}).wait_recv()
         for way in range(2):
             c = hop(far, r, way, b)
@@ -131,7 +131,7 @@
     def q_copy(kk, sign=1):
         x_, a_, b_ = peer(kk, sign)
         return remote(
-            q.at[:, cols(x_ * 4 + b_, 16), cols(a_, 512)], q_recv.at[mine], q_s.at[kk], q_r.at[kk],
+            q.at[:, cols(x_ * 4 + b_, 16), cols(a_, 512)], q_recv.at[pl.ds(2 * mine, 2)], q_s.at[kk], q_r.at[kk],
             {"ctx": ctx_of(x_, a_, b_)},
         )
 
@@ -177,7 +177,7 @@
 
     def q_wait(kk, _):
         x_, a_, b_ = peer(kk, -1)
-        at = q_recv.at[x_ * 16 + b_ * 4 + a_]
+        at = q_recv.at[pl.ds(2 * (x_ * 16 + b_ * 4 + a_), 2)]
         remote(at, at, q_s.at[kk], q_r.at[kk], {"ctx": ctx_of(x_, a_, b_)}).wait_recv()
         return 0
 
@@ -193,7 +193,7 @@
     def d_copy(kk):
         x_, a_, b_ = peer(kk, 1)
         return remote(
-            d_home.at[:, cols(x_ * 4 + b_, 16), cols(a_, 512)], d_recv.at[mine], d_s.at[kk], d_r.at[kk],
+            d_home.at[:, cols(x_ * 4 + b_, 16), cols(a_, 512)], d_recv.at[pl.ds(2 * mine, 2)], d_s.at[kk], d_r.at[kk],
             {"ctx": ctx_of(x_, a_, b_)},
         )
 
@@ -202,15 +202,14 @@
         return 0
 
     lax.fori_loop(1, N, d_start, 0)
-    d_recv[mine] = d_home[:, cols(t, 16), cols(a, 512)]
+    d_recv[pl.ds(2 * mine, 2)] = d_home[:, cols(t, 16), cols(a, 512)]
 
     def arrange(p, _):
-        at = order[64 + p]
-        part = order[128 + p]
+        at = where[p]
         to = pl.ds(pl.multiple_of(p * 128, 128), 128)
-        kpos[to, :] = kv[at, 0, part]
-        vp[to, :HD] = kv[at, 1, part]
-        slab = q_recv[at, part]
+        kpos[to, :] = kv[at, 0]
+        vp[to, :HD] = kv[at, 1]
+        slab = q_recv[at]
         for h in range(4):
             qp[p // 8, h, pl.ds(pl.multiple_of(lax.rem(p, 8) * 16, 16), 16), :] = slab[:, h * HD : h * HD + HD]
         return 0
@@ -218,18 +217,23 @@
     lax.fori_loop(0, 64, arrange, 0)
 
     def score(g, j, dst):
-        dst[...] = lax.dot_general(
+        s = lax.dot_general(
             qp[g].reshape(M, HD), kpos[cols(j, CW), :], (((1,), (1,)), ((), ())), preferred_element_type=F32
         )
+        dst[...] = s
+        top = ma if dst is sa else mb
+        top[...] = jnp.broadcast_to(jnp.max(s, axis=1, keepdims=True), (M, 128))
 
     def absorb(src, j, diagonal=False):
         s = src[...]
+        top = (ma if src is sa else mb)[...]
         if diagonal:
             row = lax.rem(lax.broadcasted_iota(jnp.int32, (M, CW), 0), 128)
             col = lax.broadcasted_iota(jnp.int32, (M, CW), 1)
             s = jnp.where(col <= (row // 16) * 128 + t * 16 + lax.rem(row, 16), s, NEG)
+            top = jnp.max(s, axis=1, keepdims=True)
         old = m_ref[...]
-        new = jnp.maximum(old, jnp.max(s, axis=1, keepdims=True))
+        new = jnp.maximum(old, top)
         m_ref[...] = new
         factor = jnp.exp2((old - new) * SCALE)
         p = jnp.exp2(s * SCALE - jnp.tile(new * SCALE, (1, CW // 128))).astype(BF16)
@@ -290,14 +294,14 @@
 
     def d_wait(kk, _):
         x_, a_, b_ = peer(kk, -1)
-        at = d_recv.at[x_ * 16 + b_ * 4 + a_]
+        at = d_recv.at[pl.ds(2 * (x_ * 16 + b_ * 4 + a_), 2)]
         remote(at, at, d_s.at[kk], d_r.at[kk], {"ctx": ctx_of(x_, a_, b_)}).wait_recv()
         return 0
 
     lax.fori_loop(1, N, d_wait, 0)
 
     def arrange_d(p, _):
-        dpos[cols(p, 16), :] = d_recv[order[64 + p], order[128 + p]]
+        dpos[cols(p, 16), :] = d_recv[where[p]]
         return 0
 
     lax.fori_loop(0, 64, arrange_d, 0)
@@ -319,7 +323,7 @@
     lax.fori_loop(0, 4, project, 0)
 
     def arrange_sh(blk, _):
-        sh_send[blk // 2, lax.rem(blk, 2)] = aw[order[blk]]
+        sh_send[blk // 2, lax.rem(blk, 2)] = aw[pos[blk]]
         return 0
 
     lax.fori_loop(0, 64, arrange_sh, 0)
@@ -433,14 +437,18 @@
                 wb_copy(da, far).wait_send()
 
 
+def add_up(li, sh, wg, hidden, grad):
+    hidden[...] = (li[...].astype(F32) + sh[...].astype(F32)).astype(BF16)
+    grad[...] = wg[0].astype(F32) + wg[1].astype(F32)
+
+
 def local(query_states, key_states, value_states, layer_inputs, out_weight, teacher, teacher_map, offsets):
-    pos = offsets // 128
-    ids = jnp.arange(64, dtype=jnp.int32)
-    inv = jnp.sum(jnp.where(pos[None, :] == ids[:, None], ids[None, :], 0), axis=1)
-    home = inv // 2
+    pos = lax.shift_right_logical(offsets, 7)
+    blk = lax.iota(jnp.int32, 64)
+    home, part = blk // 2, blk % 2
     swapped = (home // 16) * 16 + (home % 4) * 4 + (home // 4) % 4
-    slot = jnp.where(lax.axis_index("student") % 2 == 0, home, swapped)
-    order = jnp.concatenate([pos, slot, inv % 2])
+    slot = jnp.where(lax.axis_index("student") % 2 == 0, home, swapped) * 2 + part
+    where = jnp.sum(jnp.where(pos[None, :] == blk[:, None], slot[None, :], 0), axis=1)
     hbm = pl.BlockSpec(memory_space=pl.ANY)
     vmem = pl.BlockSpec(memory_space=pltpu.VMEM)
     dma = pltpu.SemaphoreType.DMA
@@ -451,21 +459,21 @@
             jax.ShapeDtypeStruct((2, 128, 2048), BF16),
             jax.ShapeDtypeStruct((2, 64, 2048), BF16),
         ),
-        in_specs=[hbm] * 7 + [pl.BlockSpec(memory_space=pltpu.SMEM)],
+        in_specs=[hbm] * 7 + [pl.BlockSpec(memory_space=pltpu.SMEM)] * 2,
         out_specs=(vmem, vmem),
         scratch_shapes=[
             pltpu.VMEM((2, 128, 2048), BF16),
             pltpu.VMEM((2048, 512), BF16),
             pltpu.VMEM((256, 2048), BF16),
             pltpu.VMEM((2, 2048, 512), BF16),
-            pltpu.VMEM((32, 2, 2, 128, 128), BF16),
-            pltpu.VMEM((32, 2, 16, 512), BF16),
+            pltpu.VMEM((64, 2, 128, 128), BF16),
+            pltpu.VMEM((64, 16, 512), BF16),
             pltpu.VMEM((GROUPS, 4, 128, 128), BF16),
             pltpu.VMEM((8192, 128), BF16),
             pltpu.VMEM((8192, 256), BF16),
             pltpu.VMEM((1024, 2048), BF16),
             pltpu.VMEM((2, 128, 2048), BF16),
-            pltpu.VMEM((32, 2, 16, 512), BF16),
+            pltpu.VMEM((64, 16, 512), BF16),
             pltpu.VMEM((1024, 512), BF16),
             pltpu.VMEM((256, 2048), F32),
             pltpu.VMEM((128, 2048), F32),
@@ -481,6 +489,8 @@
             pltpu.VMEM((M, CW), F32),
             pltpu.VMEM((M, CW), F32),
             pltpu.VMEM((M, 128), F32),
+            pltpu.VMEM((M, 128), F32),
+            pltpu.VMEM((M, 128), F32),
             pltpu.VMEM((M, 256), F32),
             dma((6,)), dma((2,)),
             dma((2, 4, 2)), dma((2, 4, 2)),
@@ -494,10 +504,24 @@
         ),
     )(
         query_states[0].reshape(2, 128, 2048), key_states[0].reshape(2, 128, 512), value_states[0].reshape(2, 128, 512),
-        layer_inputs[0].reshape(2, 128, 2048), out_weight[0], teacher, teacher_map, order,
+        layer_inputs[0].reshape(2, 128, 2048), out_weight[0], teacher, teacher_map, pos, where,
     )
-    hidden = (layer_inputs[0].astype(F32) + sh.reshape(256, 2048).astype(F32)).astype(BF16)
-    return hidden[None], (wg[0].astype(F32) + wg[1].astype(F32))[None]
+    hidden, grad = pl.pallas_call(
+        add_up,
+        name="add_up",
+        grid=(4,),
+        out_shape=(jax.ShapeDtypeStruct((256, 2048), BF16), jax.ShapeDtypeStruct((64, 2048), F32)),
+        in_specs=[
+            pl.BlockSpec((64, 2048), lambda i: (i, 0)),
+            pl.BlockSpec((64, 2048), lambda i: (i, 0)),
+            pl.BlockSpec((2, 16, 2048), lambda i: (0, i, 0)),
+        ],
+        out_specs=(
+            pl.BlockSpec((64, 2048), lambda i: (i, 0)),
+            pl.BlockSpec((16, 2048), lambda i: (i, 0)),
+        ),
+    )(layer_inputs[0], sh.reshape(256, 2048), wg)
+    return hidden[None], grad[None]
 
 
 def solution(mesh):

time: 130 us -> 129 us (level)
  other arithmetic: 4.94 us -> 1.3 us
  Pallas kernels: 124 us -> 126 us
    pallas_call x0 -> x1, Pallas kernels: none -> 3.79 us  [local(): pl.pallas_call(add_up, name='add_up', grid=(4,), out_shape=(jax.ShapeDtyp...]
    convert_element_type x1 -> x0, other arithmetic: 2.65 us -> none  [local(): (layer_inputs[0].astype(F32) + sh.reshape(256, 2048).astype(F32)).astype(...]
    pallas_call x1, Pallas kernels: 124 us -> 122 us  [local(): pl.pallas_call(kernel, name='layer', out_shape=(jax.ShapeDtypeStruct((2,...]
where the time goes in v4:
time: 129 us; the launch traced here: 128 us
  Pallas kernels  126 us (98%)
  other arithmetic  1.3 us (1%)
    pallas_call x1, Pallas kernels, local(): pl.pallas_call(kernel, name='layer', out_shape=(jax.ShapeDtypeStruct((2,...  122 us
    pallas_call x1, Pallas kernels, local(): pl.pallas_call(add_up, name='add_up', grid=(4,), out_shape=(jax.ShapeDtyp...  3.79 us

profile of v4, /device:TPU:2, one launch (start us, length us, event | category | flops | bytes accessed | tf_op | source)
XLA Modules:
  0.0 128.2 jit_solution(196714380031880431)
XLA Ops:
  0.6 0.7 fusion
  1.3 0.0 copy-start
  1.3 0.6 select_reduce_fusion.where
  2.0 0.0 copy-done
  2.0 122.5 %layer.1 = (bf16[2,128,2048]{2,1,0:T(8,128)(2,1)}, bf16[2,64,2048]{2,1,0:T(8,128)(2,1)}) custom-call(bf16[2,128,2048]{2,1,0:T(8,128)(2,1)} %bitcast.12, bf16[2,128,512]{2,1,0:T(8,128)(2,1)} %bitcast.14, bf16[2,128,512]{2,1,0:T(8,128)(2,1)} %bitcast.15, bf16[2,128,2048]{2,1,0:T(8,128)(2,1)} %bitcast.10, bf16[2048,2048]{1,0:T(8,128)(2,1)} %bitcast.9, ...), custom_call_target="tpu_custom_call" | custom-call | tf_op jit(solution)/shard_map/layer/pallas_call | solution.py:455
  124.5 3.8 %add_up.1 = (bf16[256,2048]{1,0:T(8,128)(2,1)}, f32[64,2048]{1,0:T(8,128)}) custom-call(bf16[256,2048]{1,0:T(8,128)(2,1)} %bitcast.11, bf16[256,2048]{1,0:T(8,128)(2,1)} %bitcast.13, bf16[2,64,2048]{2,1,0:T(8,128)(2,1)} %get-tuple-element.7.wg), custom_call_target="tpu_custom_call" | custom-call | tf_op jit(solution)/shard_map/add_up/pallas_call | solution.py:509
Async XLA Ops:
  1.3 0.6 copy-start

commit v5 on v4

--- a/solution.py
+++ b/solution.py
@@ -204,17 +204,19 @@
     lax.fori_loop(1, N, d_start, 0)
     d_recv[pl.ds(2 * mine, 2)] = d_home[:, cols(t, 16), cols(a, 512)]
 
-    def arrange(p, _):
-        at = where[p]
-        to = pl.ds(pl.multiple_of(p * 128, 128), 128)
-        kpos[to, :] = kv[at, 0]
-        vp[to, :HD] = kv[at, 1]
-        slab = q_recv[at]
-        for h in range(4):
-            qp[p // 8, h, pl.ds(pl.multiple_of(lax.rem(p, 8) * 16, 16), 16), :] = slab[:, h * HD : h * HD + HD]
-        return 0
-
-    lax.fori_loop(0, 64, arrange, 0)
+    def arrange(eight, _):
+        for i in range(8):
+            p = eight * 8 + i
+            at = where[p]
+            to = pl.ds(pl.multiple_of(p * 128, 128), 128)
+            kpos[to, :] = kv[at, 0]
+            vp[to, :HD] = kv[at, 1]
+            slab = q_recv[at]
+            for h in range(4):
+                qp[eight, h, 16 * i : 16 * i + 16, :] = slab[:, h * HD : h * HD + HD]
+        return 0
+
+    lax.fori_loop(0, 8, arrange, 0)
 
     def score(g, j, dst):
         s = lax.dot_general(
@@ -300,11 +302,13 @@
 
     lax.fori_loop(1, N, d_wait, 0)
 
-    def arrange_d(p, _):
-        dpos[cols(p, 16), :] = d_recv[where[p]]
-        return 0
-
-    lax.fori_loop(0, 64, arrange_d, 0)
+    def arrange_d(eight, _):
+        for i in range(8):
+            p = eight * 8 + i
+            dpos[cols(p, 16), :] = d_recv[where[p]]
+        return 0
+
+    lax.fori_loop(0, 8, arrange_d, 0)
     c_w.wait()
 
     def project(i, _):
@@ -322,11 +326,12 @@
 
     lax.fori_loop(0, 4, project, 0)
 
-    def arrange_sh(blk, _):
-        sh_send[blk // 2, lax.rem(blk, 2)] = aw[pos[blk]]
-        return 0
-
-    lax.fori_loop(0, 64, arrange_sh, 0)
+    def arrange_sh(eight, _):
+        for i in range(8):
+            sh_send[eight * 4 + i // 2, i % 2] = aw[pos[eight * 8 + i]]
+        return 0
+
+    lax.fori_loop(0, 8, arrange_sh, 0)
 
     def sh_copy(kk):
         x_, a_, b_ = peer(kk, 1)
@@ -366,6 +371,22 @@
         for db in range(1, 4):
             wa_copy(x_, db).start()
 
+    for c in sent:
+        c.wait_send()
+
+    def drain(kk, _):
+        q_copy(kk).wait_send()
+        d_copy(kk).wait_send()
+        return 0
+
+    lax.fori_loop(1, N, drain, 0)
+
+    def drain_att(g, _):
+        for da in range(1, 4):
+            att_copy(g, da).wait_send()
+        return 0
+
+    lax.fori_loop(0, GROUPS, drain_att, 0)
     def wb_copy(da, far):
         to = lax.rem(a + da, 4)
         x_ = xo if far else xh
@@ -400,6 +421,12 @@
         return 0
 
     lax.fori_loop(1, N, sh_wait, 0)
+
+    def sh_drain(kk, _):
+        sh_copy(kk).wait_send()
+        return 0
+
+    lax.fori_loop(1, N, sh_drain, 0)
     for far in (1, 0):
         x_ = xo if far else xh
         for da in range(4):
@@ -411,23 +438,6 @@
                 {"ctx": ctx_of(x_, frm, b)},
             ).wait_recv()
 
-    for c in sent:
-        c.wait_send()
-
-    def drain(kk, _):
-        q_copy(kk).wait_send()
-        d_copy(kk).wait_send()
-        sh_copy(kk).wait_send()
-        return 0
-
-    lax.fori_loop(1, N, drain, 0)
-
-    def drain_att(g, _):
-        for da in range(1, 4):
-            att_copy(g, da).wait_send()
-        return 0
-
-    lax.fori_loop(0, GROUPS, drain_att, 0)
     for x_ in (xo, xh):
         for db in range(1, 4):
             wa_copy(x_, db).wait_send()

time: 129 us -> 128 us (level)
  no operation moved by 1% of the time
where the time goes in v5:
time: 128 us; the launch traced here: 127 us
  Pallas kernels  125 us (98%)
  other arithmetic  1.3 us (1%)
    pallas_call x1, Pallas kernels, local(): pl.pallas_call(kernel, name='layer', out_shape=(jax.ShapeDtypeStruct((2,...  121 us
    pallas_call x1, Pallas kernels, local(): pl.pallas_call(add_up, name='add_up', grid=(4,), out_shape=(jax.ShapeDtyp...  3.79 us

profile of v5, /device:TPU:2, one launch (start us, length us, event | category | flops | bytes accessed | tf_op | source)
XLA Modules:
  0.0 127.0 jit_solution(7687561388839929650)
XLA Ops:
  0.6 0.7 fusion
  1.3 0.0 copy-start
  1.3 0.6 select_reduce_fusion.where
  2.0 0.0 copy-done
  2.0 121.2 %layer.1 = (bf16[2,128,2048]{2,1,0:T(8,128)(2,1)}, bf16[2,64,2048]{2,1,0:T(8,128)(2,1)}) custom-call(bf16[2,128,2048]{2,1,0:T(8,128)(2,1)} %bitcast.12, bf16[2,128,512]{2,1,0:T(8,128)(2,1)} %bitcast.14, bf16[2,128,512]{2,1,0:T(8,128)(2,1)} %bitcast.15, bf16[2,128,2048]{2,1,0:T(8,128)(2,1)} %bitcast.10, bf16[2048,2048]{1,0:T(8,128)(2,1)} %bitcast.9, ...), custom_call_target="tpu_custom_call" | custom-call | tf_op jit(solution)/shard_map/layer/pallas_call | solution.py:465
  123.2 3.8 %add_up.1 = (bf16[256,2048]{1,0:T(8,128)(2,1)}, f32[64,2048]{1,0:T(8,128)}) custom-call(bf16[256,2048]{1,0:T(8,128)(2,1)} %bitcast.11, bf16[256,2048]{1,0:T(8,128)(2,1)} %bitcast.13, bf16[2,64,2048]{2,1,0:T(8,128)(2,1)} %get-tuple-element.7.wg), custom_call_target="tpu_custom_call" | custom-call | tf_op jit(solution)/shard_map/add_up/pallas_call | solution.py:519
Async XLA Ops:
  1.3 0.6 copy-start

commit v6 on v5

--- a/solution.py
+++ b/solution.py
@@ -213,7 +213,7 @@
             vp[to, :HD] = kv[at, 1]
             slab = q_recv[at]
             for h in range(4):
-                qp[eight, h, 16 * i : 16 * i + 16, :] = slab[:, h * HD : h * HD + HD]
+                qp[eight, i // 4 * 4 + h, 16 * (i % 4) : 16 * (i % 4) + 16, :] = slab[:, h * HD : h * HD + HD]
         return 0
 
     lax.fori_loop(0, 8, arrange, 0)
@@ -226,22 +226,28 @@
         top = ma if dst is sa else mb
         top[...] = jnp.broadcast_to(jnp.max(s, axis=1, keepdims=True), (M, 128))
 
+    def update(first, s, top, keys):
+        rows = pl.ds(first, M - first)
+        old = m_ref[rows, :]
+        new = jnp.maximum(old, top)
+        m_ref[rows, :] = new
+        factor = jnp.exp2((old - new) * SCALE)
+        p = jnp.exp2(s * SCALE - jnp.tile(new * SCALE, (1, s.shape[1] // 128))).astype(BF16)
+        acc[rows, :] = acc[rows, :] * jnp.tile(factor, (1, 2)) + jnp.dot(
+            p, vp[keys, :], preferred_element_type=F32
+        )
+
     def absorb(src, j, diagonal=False):
-        s = src[...]
-        top = (ma if src is sa else mb)[...]
-        if diagonal:
-            row = lax.rem(lax.broadcasted_iota(jnp.int32, (M, CW), 0), 128)
-            col = lax.broadcasted_iota(jnp.int32, (M, CW), 1)
-            s = jnp.where(col <= (row // 16) * 128 + t * 16 + lax.rem(row, 16), s, NEG)
-            top = jnp.max(s, axis=1, keepdims=True)
-        old = m_ref[...]
-        new = jnp.maximum(old, top)
-        m_ref[...] = new
-        factor = jnp.exp2((old - new) * SCALE)
-        p = jnp.exp2(s * SCALE - jnp.tile(new * SCALE, (1, CW // 128))).astype(BF16)
-        acc[...] = acc[...] * jnp.tile(factor, (1, 2)) + jnp.dot(
-            p, vp[cols(j, CW), :], preferred_element_type=F32
-        )
+        if not diagonal:
+            update(0, src[...], (ma if src is sa else mb)[...], cols(j, CW))
+            return
+        row = lax.broadcasted_iota(jnp.int32, (256, 512), 0)
+        col = lax.broadcasted_iota(jnp.int32, (256, 512), 1)
+        ok = col <= (lax.rem(row, 64) // 16) * 128 + t * 16 + lax.rem(row, 16)
+        s = jnp.concatenate([jnp.where(ok, src[:256, :512], NEG), src[256:, :512]], axis=0)
+        update(0, s, jnp.max(s, axis=1, keepdims=True), cols(2 * j, 512))
+        s = jnp.where(ok, src[256:, 512:], NEG)
+        update(256, s, jnp.max(s, axis=1, keepdims=True), cols(2 * j + 1, 512))
 
     def begin():
         m_ref[...] = jnp.full((M, 128), NEG, F32)
@@ -252,9 +258,10 @@
         return remote(at, at, ag_s.at[g, da], ag_r.at[g, da], {"ctx": ctx_of(xh, lax.rem(a + da, 4), b)})
 
     def finish(g):
-        for h in range(4):
-            rows = slice(h * 128, h * 128 + 128)
-            att[cols(g, 128), pl.ds(pl.multiple_of(a * 512 + h * 128, 128), 128)] = (
+        for i in range(8):
+            rows = slice(i * 64, i * 64 + 64)
+            to = pl.ds(pl.multiple_of(g * 128 + i // 4 * 64, 64), 64)
+            att[to, pl.ds(pl.multiple_of(a * 512 + i % 4 * 128, 128), 128)] = (
                 acc[rows, :HD] / acc[rows, HD:]
             ).astype(BF16)
         for da in range(1, 4):
@@ -478,7 +485,7 @@
             pltpu.VMEM((2, 2048, 512), BF16),
             pltpu.VMEM((64, 2, 128, 128), BF16),
             pltpu.VMEM((64, 16, 512), BF16),
-            pltpu.VMEM((GROUPS, 4, 128, 128), BF16),
+            pltpu.VMEM((GROUPS, 8, 64, 128), BF16),
             pltpu.VMEM((8192, 128), BF16),
             pltpu.VMEM((8192, 256), BF16),
             pltpu.VMEM((1024, 2048), BF16),

time: 128 us -> 128 us (level)
  no operation moved by 1% of the time
where the time goes in v6:
time: 128 us; the launch traced here: 127 us
  Pallas kernels  125 us (98%)
  other arithmetic  1.3 us (1%)
    pallas_call x1, Pallas kernels, local(): pl.pallas_call(kernel, name='layer', out_shape=(jax.ShapeDtypeStruct((2,...  121 us
    pallas_call x1, Pallas kernels, local(): pl.pallas_call(add_up, name='add_up', grid=(4,), out_shape=(jax.ShapeDtyp...  3.79 us

profile of v6, /device:TPU:2, one launch (start us, length us, event | category | flops | bytes accessed | tf_op | source)
XLA Modules:
  0.0 126.9 jit_solution(13630183591769097458)
XLA Ops:
  0.6 0.7 fusion
  1.3 0.0 copy-start
  1.3 0.6 select_reduce_fusion.where
  2.0 0.0 copy-done
  2.0 121.2 %layer.1 = (bf16[2,128,2048]{2,1,0:T(8,128)(2,1)}, bf16[2,64,2048]{2,1,0:T(8,128)(2,1)}) custom-call(bf16[2,128,2048]{2,1,0:T(8,128)(2,1)} %bitcast.12, bf16[2,128,512]{2,1,0:T(8,128)(2,1)} %bitcast.14, bf16[2,128,512]{2,1,0:T(8,128)(2,1)} %bitcast.15, bf16[2,128,2048]{2,1,0:T(8,128)(2,1)} %bitcast.10, bf16[2048,2048]{1,0:T(8,128)(2,1)} %bitcast.9, ...), custom_call_target="tpu_custom_call" | custom-call | tf_op jit(solution)/shard_map/layer/pallas_call | solution.py:472
  123.1 3.8 %add_up.1 = (bf16[256,2048]{1,0:T(8,128)(2,1)}, f32[64,2048]{1,0:T(8,128)}) custom-call(bf16[256,2048]{1,0:T(8,128)(2,1)} %bitcast.11, bf16[256,2048]{1,0:T(8,128)(2,1)} %bitcast.13, bf16[2,64,2048]{2,1,0:T(8,128)(2,1)} %get-tuple-element.7.wg), custom_call_target="tpu_custom_call" | custom-call | tf_op jit(solution)/shard_map/add_up/pallas_call | solution.py:526
Async XLA Ops:
  1.3 0.6 copy-start
